TPU v7x, 32 devices: a whole 2x2x4 slice. The times are simulated.
32 devices in a mesh: batch: 4 (over y, core), seq: 8 (over z, x).
Axes of the slice: x: 2, y: 2, z: 4, core: 2. Of those that a mesh axis runs over, the one named last changes fastest.
Arguments:
- values: bfloat16 [1024, 8192], P(None, ('batch', 'seq')), may hold values from -6 to 6
- gates: bfloat16 [1024, 8192], P(None, ('batch', 'seq')), may hold values from -6 to 6
- cotangent: bfloat16 [1024, 8192], P(None, ('batch', 'seq')), may hold values from -12 to 12
- taps_values: float32 [3, 1024], replicated, may hold values from -3 to 3
- taps_gates: float32 [3, 1024], replicated, may hold values from -3 to 3
- skip_gain: float32 [1024], replicated, may hold values from 0.5 to 1.5
- twiddle: float32 [8, 1024], P('batch'), may hold values from 0.5 to 1.5
- mixing: float32 [8, 8], replicated, may hold values from -2 to 3
- spectrum: bfloat16 [1024, 8, 1024], P('seq', None, 'batch'), may hold values from -4 to 4
Outputs:
- mixed: bfloat16 [1024, 8192], P(None, ('batch', 'seq'))
- grad_values: bfloat16 [1024, 8192], P(None, ('batch', 'seq'))
- grad_gates: bfloat16 [1024, 8192], P(None, ('batch', 'seq'))
- grad_spectrum: float32 [1024, 8, 1024], P('seq', None, 'batch')
- grad_taps_values: float32 [3, 1024], P(None, 'seq')
- grad_taps_gates: float32 [3, 1024], P(None, 'seq')
- grad_skip: float32 [1024], P('seq')
All inputs are finite; a program needn't handle non-finite values.
Results may differ from a plain program's by a relative error of at most 0.0085.
Values may be sent and summed in bfloat16 or wider, within the bound.
A program may use at most 64 MiB of HBM per device.

v0:
```python
import math

import jax
import jax.numpy as jnp
import numpy as np
from jax import lax
from jax.sharding import PartitionSpec as P

AXES = ("batch", "seq")


def cas_table(block):
    angles = np.arange(block, dtype=np.float32) * np.float32(2.0 * math.pi / block)
    entries = (np.cos(angles) + np.sin(angles)) / np.float32(math.sqrt(block))
    indices = np.arange(block)
    return jnp.asarray(entries.astype(jnp.bfloat16)[indices[:, None] * indices[None, :] % block])


def delayed(field, steps):
    return jnp.pad(field, ((0, 0), (steps, 0)))[:, : field.shape[1]]


def advanced(field, steps):
    return jnp.pad(field, ((0, 0), (0, steps)))[:, steps:]


def short_conv(field, taps, shift):
    return (
        taps[0][:, None] * field
        + taps[1][:, None] * shift(field, 1)
        + taps[2][:, None] * shift(field, 2)
    )


def tap_sums(gradient, field):
    return jnp.stack([jnp.sum(gradient * delayed(field, s), axis=1) for s in range(3)])


def per_device_plain(
    values, gates, cotangent, taps_values, taps_gates, skip_gain, twiddle, mixing, spectrum
):
    block = twiddle.shape[1]
    cas = cas_table(block)
    batch, seq = lax.axis_size("batch"), lax.axis_size("seq")
    share = values.shape[0] // (batch * seq)
    b, s = lax.axis_index("batch"), lax.axis_index("seq")
    start = (s * batch + b) * share
    stacked = jnp.stack([values, gates, cotangent])
    length_dev = values.shape[1]
    stacked = stacked.reshape(3, seq, batch, share, length_dev).transpose(2, 1, 0, 3, 4)
    stacked = stacked.reshape(batch * seq, 3, share, length_dev)
    whole = lax.all_to_all(stacked, AXES, split_axis=0, concat_axis=0, tiled=True)
    whole = whole.transpose(1, 2, 0, 3).reshape(3, share, -1)
    filters = lax.all_to_all(spectrum, "batch", split_axis=0, concat_axis=2, tiled=True)
    filters = filters.astype(jnp.float32)
    factors = lax.all_gather(twiddle, "batch", axis=0, tiled=True)
    params = jnp.concatenate([taps_values, taps_gates, skip_gain[None]], axis=0)
    params = lax.dynamic_slice_in_dim(params, start, share, 1)
    value_taps, gate_taps, skip = params[:3], params[3:6], params[6][:, None]
    field, gate, cot = (whole[n].astype(jnp.float32) for n in range(3))
    short_values = short_conv(field, value_taps, delayed).astype(jnp.bfloat16)
    short_gates = short_conv(gate, gate_taps, delayed)
    grad_long = (cot * short_gates).astype(jnp.bfloat16)

    def transform(source):
        sums = jnp.dot(source.reshape(-1, block), cas, preferred_element_type=jnp.float32)
        sums = sums.reshape(share, -1, block) * factors
        return jnp.einsum("pi,cik->cpk", mixing, sums, precision=lax.Precision.HIGHEST)

    def back(spectra):
        mixed = jnp.einsum("pi,cpk->cik", mixing, spectra, precision=lax.Precision.HIGHEST)
        weighted = (mixed * factors).astype(jnp.bfloat16)
        result = jnp.dot(weighted.reshape(-1, block), cas, preferred_element_type=jnp.float32)
        return result.reshape(share, -1).astype(jnp.bfloat16).astype(jnp.float32)

    spectra_values, spectra_grads = transform(short_values), transform(grad_long)
    long_values, back_grads = back(spectra_values * filters), back(spectra_grads * filters)
    grad_spectrum = (spectra_values * spectra_grads).astype(jnp.bfloat16)
    grad_spectrum = lax.all_to_all(grad_spectrum, "batch", split_axis=2, concat_axis=0, tiled=True)
    short_f32 = short_values.astype(jnp.float32)
    long_f32 = grad_long.astype(jnp.float32)
    inner = long_values + skip * short_f32
    grad_short_gates = cot * inner
    grad_short_values = skip * long_f32 + back_grads
    outs = jnp.stack([
        (short_gates * inner).astype(jnp.bfloat16),
        short_conv(grad_short_values, value_taps, advanced).astype(jnp.bfloat16),
        short_conv(grad_short_gates, gate_taps, advanced).astype(jnp.bfloat16),
    ])
    outs = outs.reshape(3, share, batch * seq, length_dev).transpose(2, 0, 1, 3)
    outs = lax.all_to_all(outs, AXES, split_axis=0, concat_axis=0, tiled=True)
    outs = outs.reshape(batch, seq, 3, share, length_dev).transpose(2, 1, 0, 3, 4)
    outs = outs.reshape(3, -1, length_dev)
    sums = jnp.concatenate([
        tap_sums(grad_short_values, field),
        tap_sums(grad_short_gates, gate),
        jnp.sum(long_f32 * short_f32, axis=1)[None],
    ])
    sums = lax.all_gather(sums, "batch", axis=1, tiled=True)
    return (
        outs[0], outs[1], outs[2], grad_spectrum.astype(jnp.float32), sums[:3], sums[3:6], sums[6]
    )


def solution(mesh):
    spread = P(None, AXES)
    in_specs = (
        spread, spread, spread, P(), P(), P(), P("batch", None), P(), P("seq", None, "batch")
    )
    out_specs = (
        spread, spread, spread, P("seq", None, "batch"), P(None, "seq"), P(None, "seq"), P("seq")
    )
    return jax.shard_map(
        per_device_plain, mesh=mesh, in_specs=in_specs, out_specs=out_specs, check_vma=False
    )
```

profile of v0, /device:TPU:0, one launch (start us, length us, event | category | flops | bytes accessed | tf_op | source)
XLA Modules:
  0.0 148.6 jit_solution(16431195920021598959)
XLA Ops:
  0.6 0.0 copy-start
  0.6 4.2 %all-to-all-start.1 = ((bf16[128,8,256]{2,1,0:T(8,128)(2,1)}), bf16[128,8,256]{2,1,0:T(8,128)(2,1)S(1)}, u32[]{:S(2)}, u32[]{:S(2)}) async-start(bf16[128,8,256]{2,1,0:T(8,128)(2,1)} %param.18), calls=%async_computation.1 | async-start | bytes 1048576 | tf_op jit(solution)/shard_map/all_to_all | solution.py:54
  4.9 1.5 %maximum_bitcast_fusion = bf16[4,8,3,32,256]{4,3,0,1,2:T(8,128)(2,1)S(1)} fusion(bf16[1,8,4,32,256]{4,3,2,1,0:T(8,128)(2,1)} %bitcast.160, bf16[1,8,4,32,256]{4,3,2,1,0:T(8,128)(2,1)} %bitcast.161, bf16[1,8,4,32,256]{4,3,2,1,0:T(8,128)(2,1)} %bitcast.162), kind=kLoop, calls=%fused_computation.1 | loop fusion | flops 1572864 | bytes 3145728 | tf_op jit(solution)/shard_map/transpose | solution.py:50
  6.4 1.3 copy.53
  7.7 6.0 %all-to-all-done.1 = bf16[128,8,256]{2,1,0:T(8,128)(2,1)S(1)} async-done(((bf16[128,8,256]{2,1,0:T(8,128)(2,1)}), bf16[128,8,256]{2,1,0:T(8,128)(2,1)S(1)}, u32[]{:S(2)}, u32[]{:S(2)}) %all-to-all-start.1) | async-done | bytes 524320 | tf_op jit(solution)/shard_map/all_to_all | solution.py:54
  13.8 5.6 %all-to-all-start = ((bf16[32,3,32,256]{3,2,1,0:T(8,128)(2,1)}), bf16[32,3,32,256]{3,2,1,0:T(8,128)(2,1)S(1)}, u32[]{:S(2)}, u32[]{:S(2)}) async-start(bf16[32,3,32,256]{3,2,1,0:T(8,128)(2,1)} %bitcast.6), calls=%async_computation | async-start | bytes 3145728 | tf_op jit(solution)/shard_map/all_to_all | solution.py:52
  19.3 0.0 copy-done.8
  19.3 11.5 %all-gather = f32[4,2,1024]{2,1,0:T(2,128)S(1)} all-gather(f32[1,2,1024]{2,1,0:T(2,128)S(1)} %bitcast.166), channel_id=1, replica_groups=mesh['batch'=4,'seq'=8] {'batch'}, dimensions={0}, use_global_device_ids=true | all-gather | bytes 40960 | tf_op jit(solution)/shard_map/all_gather | solution.py:56
  30.9 0.0 copy-done.6
  30.9 0.0 copy-done.7
  30.9 0.0 copy-done.9
  30.9 0.1 fusion.25
  31.0 1.1 copy.56
  32.1 26.0 %all-to-all-done = bf16[32,3,32,256]{3,2,1,0:T(8,128)(2,1)S(1)} async-done(((bf16[32,3,32,256]{3,2,1,0:T(8,128)(2,1)}), bf16[32,3,32,256]{3,2,1,0:T(8,128)(2,1)S(1)}, u32[]{:S(2)}, u32[]{:S(2)}) %all-to-all-start) | async-done | bytes 1572896 | tf_op jit(solution)/shard_map/all_to_all | solution.py:52
  58.1 0.4 slice_convert_fusion.1
  58.6 0.1 copy.72
  58.6 0.1 copy.75
  58.7 0.1 copy.71
  58.8 2.2 %fusion.20 = (f32[32]{0:T(128)S(1)}, bf16[32,8192]{1,0:T(8,128)(2,1)S(1)}, f32[32,8192]{1,0:T(8,128)}, bf16[32,8192]{1,0:T(8,128)(2,1)S(1)}) fusion(f32[32,8192]{1,0:T(8,128)S(1)} %bitcast.133, f32[32,8192]{1,0:T(8,128)S(1)} %bitcast.135, f32[32]{0:T(128)S(1)} %get-tuple-element.32, f32[32]{0:T(128)S(1)} %get-tuple-element.33, f32[32]{0:T(128)S(1)} %get-tuple-element.34, ...), kind=kLoop, calls=%fused_computation.42 | loop fusion | flops 4456416 | bytes 5243776 | tf_op jit(solution)/shard_map/reduce_sum | solution.py:97
  61.1 0.0 copy-start.5
  61.1 0.0 copy-start.3
  61.1 0.3 copy.73
  61.4 0.3 copy.76
  61.7 1.4 copy-done.3
  63.1 0.7 convolution_multiply_fusion.1
  63.8 0.0 copy-done.4
  63.8 0.0 copy-done.5
  63.8 0.7 convolution_multiply_fusion
  64.5 0.0 copy-done
  64.6 0.0 copy-start.1
  64.6 1.0 convolution_bitcast_fusion.1
  65.6 0.2 copy-done.1
  65.8 1.9 %fusion.6 = bf16[256,1024]{1,0:T(8,128)(2,1)} fusion(f32[32,8,1024]{2,1,0:T(8,128)S(1)} %convolution_bitcast_fusion.1, f32[32,8,1024]{2,1,0:T(8,128)S(1)} %bitcast.137, f32[8,1024]{1,0:T(8,128)S(1)} %reshape.106, f32[8,8]{1,0:T(8,128)S(1)} %copy-done), kind=kOutput, calls=%fused_computation.20 | convolution fusion | flops 25952256 | bytes 2654464 | tf_op jit(solution)/shard_map/pi,cpk->cik/dot_general | solution.py:71
  67.7 1.9 %multiply_convert_fusion = (bf16[32,8,1024]{2,1,0:T(8,128)(2,1)}, f32[32,8,1024]{2,1,0:T(8,128)S(1)}) fusion(f32[32,8,1024]{2,1,0:T(8,128)S(1)} %convolution_bitcast_fusion.1, f32[32,8,1024]{2,1,0:T(8,128)S(1)} %convolution_multiply_fusion.1, f32[8,8]{1,0:T(8,128)S(1)} %copy-done), kind=kOutput, calls=%fused_computation.49 | convolution fusion | flops 25690112 | bytes 3670272 | tf_op jit(solution)/shard_map/pi,cik->cpk/dot_general | solution.py:68
  69.6 1.1 fusion.7
  70.7 0.5 copy-done.2
  71.2 1.7 %fusion.2 = f32[256,1024]{1,0:T(8,128)} fusion(bf16[256,1024]{1,0:T(8,128)(2,1)S(1)} %fusion.7, bf16[1024,1024]{1,0:T(8,128)(2,1)S(1)} %copy-done.2), kind=kOutput, calls=%fused_computation.16 | convolution fusion | flops 537395200 | bytes 3670016 | tf_op jit(solution)/shard_map/dot_general | solution.py:73
  72.9 2.4 %reshape.99 = f32[32,8192]{1,0:T(8,128)} reshape(f32[256,1024]{1,0:T(8,128)} %fusion.2) | data formatting | bytes 2097152 | tf_op jit(solution)/shard_map/convert_element_type | solution.py:74
  75.3 3.5 %fusion.3 = f32[256,1024]{1,0:T(8,128)} fusion(bf16[256,1024]{1,0:T(8,128)(2,1)} %fusion.6, bf16[1024,1024]{1,0:T(8,128)(2,1)} %constant.21.clone), kind=kOutput, calls=%fused_computation.17 | convolution fusion | flops 537395200 | bytes 3670016 | tf_op jit(solution)/shard_map/dot_general | solution.py:73
  78.7 2.4 %reshape.101 = f32[32,8192]{1,0:T(8,128)} reshape(f32[256,1024]{1,0:T(8,128)} %fusion.3) | data formatting | bytes 2097152 | tf_op jit(solution)/shard_map/convert_element_type | solution.py:74
  81.1 3.6 %copy.64 = bf16[32,8,1024]{0,1,2:T(8,128)(2,1)} copy(bf16[32,8,1024]{2,1,0:T(8,128)(2,1)} %get-tuple-element.40) | data formatting | bytes 1048576 | tf_op jit(solution)/shard_map/convert_element_type | solution.py:78
  84.7 4.5 %reshape.113 = bf16[4,2,32768]{2,1,0:T(2,128)(2,1)} reshape(bf16[1024,8,32]{2,1,0:T(8,128)(2,1)} %bitcast.140) | data formatting | bytes 1048576
  89.2 4.3 %all-to-all-start.3 = ((bf16[4,2,32768]{2,1,0:T(2,128)(2,1)}), bf16[4,2,32768]{2,1,0:T(2,128)(2,1)}, u32[]{:S(2)}, u32[]{:S(2)}) async-start(bf16[4,2,32768]{2,1,0:T(2,128)(2,1)} %reshape.113), calls=%async_computation.3 | async-start | bytes 1048576 | tf_op jit(solution)/shard_map/all_to_all | solution.py:79
  93.6 3.8 %multiply_reduce_fusion.3 = (f32[32]{0:T(128)S(1)}, f32[32]{0:T(128)S(1)}, f32[32]{0:T(128)S(1)}, f32[32,8192]{1,0:T(8,128)S(1)}, bf16[32,8192]{1,0:T(8,128)(2,1...) fusion(f32[32,8192]{1,0:T(8,128)S(1)} %bitcast.132, f32[32,8192]{1,0:T(8,128)} %reshape.101, ...), kind=kLoop, calls=%fused_computation.46 | loop fusion | flops 5504832 | bytes 9962368 | tf_op jit(solution)/shard_map/reduce_sum | solution.py:36
  97.3 1.2 fusion.11
  98.6 0.1 copy.74
  98.7 0.1 copy.77
  98.8 0.1 copy.78
  98.9 0.2 maximum_bitcast_fusion.1
  99.1 2.1 %copy.60 = bf16[32,3,32,256]{3,2,1,0:T(8,128)(2,1)} copy(bf16[32,3,32,256]{3,0,2,1:T(8,128)(2,1)S(1)} %maximum_bitcast_fusion.1) | data formatting | bytes 3145728 | tf_op jit(solution)/shard_map/transpose | solution.py:90
  101.2 1.1 all-to-all-done.3
  102.3 3.4 %all-to-all-start.2 = ((bf16[32,3,32,256]{3,2,1,0:T(8,128)(2,1)}), bf16[32,3,32,256]{3,2,1,0:T(8,128)(2,1)}, u32[]{:S(2)}, u32[]{:S(2)}) async-start(bf16[32,3,32,256]{3,2,1,0:T(8,128)(2,1)} %copy.60), calls=%async_computation.2 | async-start | bytes 3145728 | tf_op jit(solution)/shard_map/all_to_all | solution.py:91
  105.7 11.0 %all-gather.1 = f32[4,32,7]{1,2,0:T(8,128)S(1)} all-gather(f32[1,32,7]{1,2,0:T(8,128)S(1)} %bitcast.163), channel_id=1, replica_groups=mesh['batch'=4,'seq'=8] {'batch'}, dimensions={0}, use_global_device_ids=true | all-gather | bytes 4480 | tf_op jit(solution)/shard_map/all_gather | solution.py:99
  116.7 0.1 reshape.108
  116.8 0.5 slice_bitcast_fusion
  117.3 0.6 fusion.33
  117.9 2.9 %reshape.114 = bf16[1024,8,32]{2,1,0:T(8,128)(2,1)S(1)} reshape(bf16[4,2,32768]{2,1,0:T(2,128)(2,1)} %all-to-all-done.3) | data formatting | bytes 1048576
  120.8 2.2 %convert_bitcast_fusion = f32[4,32,8,256]{1,2,3,0:T(8,128)} fusion(bf16[32,8,4,256]{0,1,3,2:T(8,128)(2,1)S(1)} %bitcast.139), kind=kLoop, calls=%fused_computation | loop fusion | flops 262144 | bytes 1572864 | tf_op jit(solution)/shard_map/convert_element_type | solution.py:101
  123.0 3.6 %copy.65 = f32[4,32,8,256]{3,2,1,0:T(8,128)} copy(f32[4,32,8,256]{1,2,3,0:T(8,128)} %convert_bitcast_fusion) | data formatting | bytes 2097152 | tf_op jit(solution)/shard_map/convert_element_type | solution.py:101
  126.6 17.9 %all-to-all-done.2 = bf16[32,3,32,256]{3,2,1,0:T(8,128)(2,1)} async-done(((bf16[32,3,32,256]{3,2,1,0:T(8,128)(2,1)}), bf16[32,3,32,256]{3,2,1,0:T(8,128)(2,1)}, u32[]{:S(2)}, u32[]{:S(2)}) %all-to-all-start.2) | async-done | bytes 1572896 | tf_op jit(solution)/shard_map/all_to_all | solution.py:91
  144.5 1.5 %fusion.32 = (bf16[1,8,4,32,256]{4,3,0,1,2:T(8,128)(2,1)S(1)}, bf16[1,8,4,32,256]{4,3,0,1,2:T(8,128)(2,1)S(1)}, bf16[1,8,4,32,256]{4,3,0,1,2:T(8,128)(2,1)S(1)}) fusion(bf16[3,8,4,32,256]{4,3,0,1,2:T(8,128)(2,1)} %bitcast.31), kind=kLoop, calls=%fused_computation.77 | loop fusion | bytes 3145728 | tf_op jit(solution)/shard_map/slice | solution.py:101
  146.0 0.8 copy.63
  146.9 0.8 copy.62
  147.7 0.8 copy.61
  (10 shorter events, 0.1 us)
Async XLA Ops:
  0.6 63.9 %copy-start = (f32[8,8]{1,0:T(8,128)S(1)}, f32[8,8]{1,0:T(8,128)}, u32[]{:S(2)}) copy-start(f32[8,8]{1,0:T(8,128)} %param.17) | copy-start | bytes 772
  0.6 13.1 %all-to-all-start.1 = ((bf16[128,8,256]{2,1,0:T(8,128)(2,1)}), bf16[128,8,256]{2,1,0:T(8,128)(2,1)S(1)}, u32[]{:S(2)}, u32[]{:S(2)}) async-start(bf16[128,8,256]{2,1,0:T(8,128)(2,1)} %param.18), calls=%async_computation.1 | async-start | bytes 1048576 | tf_op jit(solution)/shard_map/all_to_all | solution.py:54
  13.7 5.6 %copy-start.8 = (f32[2,1024]{1,0:T(2,128)S(1)}, f32[2,1024]{1,0:T(2,128)}, u32[]{:S(2)}) copy-start(f32[2,1024]{1,0:T(2,128)} %param.16) | copy-start | bytes 24580
  13.7 17.1 %copy-start.6 = (f32[3,1024]{1,0:T(4,128)S(1)}, f32[3,1024]{1,0:T(4,128)}, u32[]{:S(2)}) copy-start(f32[3,1024]{1,0:T(4,128)} %param.13) | copy-start | bytes 36868
  13.7 17.1 %copy-start.7 = (f32[3,1024]{1,0:T(4,128)S(1)}, f32[3,1024]{1,0:T(4,128)}, u32[]{:S(2)}) copy-start(f32[3,1024]{1,0:T(4,128)} %param.14) | copy-start | bytes 36868
  13.8 17.1 %copy-start.9 = (f32[1024]{0:T(1024)S(1)}, f32[1024]{0:T(1024)}, u32[]{:S(2)}) copy-start(f32[1024]{0:T(1024)} %param.15) | copy-start | bytes 12292
  13.8 44.4 %all-to-all-start = ((bf16[32,3,32,256]{3,2,1,0:T(8,128)(2,1)}), bf16[32,3,32,256]{3,2,1,0:T(8,128)(2,1)S(1)}, u32[]{:S(2)}, u32[]{:S(2)}) async-start(bf16[32,3,32,256]{3,2,1,0:T(8,128)(2,1)} %bitcast.6), calls=%async_computation | async-start | bytes 3145728 | tf_op jit(solution)/shard_map/all_to_all | solution.py:52
  61.1 2.7 %copy-start.4 = (bf16[32,8192]{1,0:T(8,128)(2,1)}, bf16[32,8192]{1,0:T(8,128)(2,1)S(1)}, u32[]{:S(2)}) copy-start(bf16[32,8192]{1,0:T(8,128)(2,1)S(1)} %get-tuple-element.14) | copy-start | bytes 1572868
  61.1 2.7 %copy-start.5 = (bf16[32,8192]{1,0:T(8,128)(2,1)}, bf16[32,8192]{1,0:T(8,128)(2,1)S(1)}, u32[]{:S(2)}) copy-start(bf16[32,8192]{1,0:T(8,128)(2,1)S(1)} %get-tuple-element.16) | copy-start | bytes 1572868
  61.1 2.0 %copy-start.3 = (bf16[1024,1024,1]{1,0,2:T(8,128)(2,1)S(1)}, bf16[1024,1024,1]{1,0,2:T(8,128)(2,1)}, u32[]{:S(2)}) copy-start(bf16[1024,1024,1]{1,0,2:T(8,128)(2,1)} %constant.39) | copy-start | bytes 6291460
  64.6 1.2 copy-start.1
  69.6 1.6 %copy-start.2 = (bf16[1024,1024]{1,0:T(8,128)(2,1)S(1)}, bf16[1024,1024]{1,0:T(8,128)(2,1)}, u32[]{:S(2)}) copy-start(bf16[1024,1024]{1,0:T(8,128)(2,1)} %constant.21.clone) | copy-start | bytes 6291460
  89.2 13.0 %all-to-all-start.3 = ((bf16[4,2,32768]{2,1,0:T(2,128)(2,1)}), bf16[4,2,32768]{2,1,0:T(2,128)(2,1)}, u32[]{:S(2)}, u32[]{:S(2)}) async-start(bf16[4,2,32768]{2,1,0:T(2,128)(2,1)} %reshape.113), calls=%async_computation.3 | async-start | bytes 1048576 | tf_op jit(solution)/shard_map/all_to_all | solution.py:79
  102.3 42.2 %all-to-all-start.2 = ((bf16[32,3,32,256]{3,2,1,0:T(8,128)(2,1)}), bf16[32,3,32,256]{3,2,1,0:T(8,128)(2,1)}, u32[]{:S(2)}, u32[]{:S(2)}) async-start(bf16[32,3,32,256]{3,2,1,0:T(8,128)(2,1)} %copy.60), calls=%async_computation.2 | async-start | bytes 3145728 | tf_op jit(solution)/shard_map/all_to_all | solution.py:91
where the time goes:
time: 149 us
  waiting for transfers between devices  51.1 us (34%)
  local copies, waits for them, and re-layouts  32.4 us (22%)
  blocking collectives  22.5 us (15%)
  starting transfers between devices  17.5 us (12%)
  matrix products  12.5 us (8%)
  other arithmetic  11.6 us (8%)
    all_to_all x1, waiting for transfers between devices, per_device_plain(): lax.all_to_all(stacked, AXES, split_axis=0, concat_axis=0, tiled=True)  26 us
    all_to_all x1, waiting for transfers between devices, per_device_plain(): outs = lax.all_to_all(outs, AXES, split_axis=0, concat_axis=0, tiled=True)  17.9 us
    all_gather x1, blocking collectives, per_device_plain(): factors = lax.all_gather(twiddle, 'batch', axis=0, tiled=True)  11.5 us
    all_gather x1, blocking collectives, per_device_plain(): sums = lax.all_gather(sums, 'batch', axis=1, tiled=True)  11 us
    unnamed x32, local copies, waits for them, and re-layouts  10.7 us
    all_to_all x1, waiting for transfers between devices, per_device_plain(): lax.all_to_all(spectrum, 'batch', split_axis=0, concat_axis=2, tiled=True)  6.01 us
    all_to_all x1, starting transfers between devices, per_device_plain(): lax.all_to_all(stacked, AXES, split_axis=0, concat_axis=0, tiled=True)  5.55 us
    dot_general x2, matrix products, back(): jnp.dot(weighted.reshape(-1, block), cas, preferred_element_type=jnp.floa...  5.15 us
  transfers between devices with their start and end apart: 4, of which 4 were waited for; matrix products, arithmetic and copies ran while one was open for 14% of the time, Pallas kernels for 0%

commit v1 on v0

--- a/solution.py
+++ b/solution.py
@@ -1,9 +1,12 @@
+import functools
 import math
 
 import jax
 import jax.numpy as jnp
 import numpy as np
 from jax import lax
+from jax.experimental import pallas as pl
+from jax.experimental.pallas import tpu as pltpu
 from jax.sharding import PartitionSpec as P
 
 AXES = ("batch", "seq")
@@ -102,6 +105,339 @@
     )
 
 
+LANES = 128
+MESH = pl.DeviceIdType.MESH
+
+
+def whole_sequences(
+    batch, seq,
+    values, gates, cotangent, spectrum, twiddle, mixing, params, cas,
+    mixed, grad_values, grad_gates, grad_spectrum, sums,
+    fields, filters, factors, short_values, grad_long, wide, weighted, spectra, filtered, gradient,
+    out_fields, out_spectrum, totals,
+    in_send, in_recv, out_send, out_recv, side_send, side_recv,
+):
+    b, s = lax.axis_index("batch"), lax.axis_index("seq")
+    count = batch * seq
+    me = b * seq + s
+    share, length = fields.shape[2], fields.shape[3]
+    block = cas.shape[0]
+    blocks = short_values.shape[0] // share
+    per_block = block // length
+    freqs = block // batch
+
+    def rows_of(bt, st):
+        return pl.ds(pl.multiple_of((st * batch + bt) * share, share), share)
+
+    def batch_rows(bt):
+        return pl.ds(pl.multiple_of(bt * share, share), share)
+
+    def other(step):
+        peer = lax.rem(me + step, count)
+        return peer, lax.div(peer, seq), lax.rem(peer, seq)
+
+    def each_other(body):
+        @pl.loop(1, count)
+        def _(step):
+            body(*other(step))
+
+    def each_batch(body):
+        for step in range(1, batch):
+            body(lax.rem(b + step, batch))
+
+    barrier = pltpu.get_barrier_semaphore()
+    each_other(lambda peer, bt, st: pl.semaphore_signal(
+        barrier, inc=1, device_id=(bt, st), device_id_type=MESH))
+    pl.semaphore_wait(barrier, count - 1)
+
+    def in_copy(n, peer, bt, st, slot):
+        return pltpu.make_async_remote_copy(
+            src_ref=(values, gates, cotangent)[n].at[rows_of(bt, st), :],
+            dst_ref=fields.at[n, me],
+            send_sem=in_send.at[n, peer],
+            recv_sem=in_recv.at[n, slot],
+            device_id=(bt, st),
+            device_id_type=MESH,
+        )
+
+    def out_copy(n, peer, bt, st, slot):
+        return pltpu.make_async_remote_copy(
+            src_ref=out_fields.at[n, peer],
+            dst_ref=(mixed, grad_gates, grad_values)[n].at[rows_of(b, s), :],
+            send_sem=out_send.at[n, peer],
+            recv_sem=out_recv.at[n, slot],
+            device_id=(bt, st),
+            device_id_type=MESH,
+        )
+
+    def side_copy(n, bt, slot):
+        source = (spectrum.at[:, batch_rows(bt), :], twiddle, out_spectrum.at[bt], sums.at[b])[n]
+        target = (filters.at[b], factors.at[b], grad_spectrum.at[:, batch_rows(b), :], sums.at[b])[n]
+        return pltpu.make_async_remote_copy(
+            src_ref=source,
+            dst_ref=target,
+            send_sem=side_send.at[n, bt],
+            recv_sem=side_recv.at[n, slot],
+            device_id=(bt, s),
+            device_id_type=MESH,
+        )
+
+    def start_in(n):
+        each_other(lambda peer, bt, st: in_copy(n, peer, bt, st, me).start())
+
+    def wait_in(n):
+        each_other(lambda peer, bt, st: in_copy(n, peer, bt, st, peer).wait_recv())
+
+    def start_out(n):
+        each_other(lambda peer, bt, st: out_copy(n, peer, bt, st, me).start())
+        (mixed, grad_gates, grad_values)[n][rows_of(b, s), :] = out_fields[n, me]
+
+    start_in(0)
+    each_batch(lambda bt: side_copy(1, bt, b).start())
+    each_batch(lambda bt: side_copy(0, bt, b).start())
+    start_in(1)
+    start_in(2)
+    for n, source in enumerate((values, gates, cotangent)):
+        fields[n, me] = source[rows_of(b, s), :]
+    filters[b] = spectrum[:, batch_rows(b), :]
+    factors[b] = twiddle[...]
+    totals[...] = jnp.zeros_like(totals)
+
+    lane = lax.broadcasted_iota(jnp.int32, (share, length), 1)
+    value_taps = [params[:, n : n + 1] for n in range(3)]
+    gate_taps = [params[:, n : n + 1] for n in range(3, 6)]
+    skip = params[:, 6:7]
+    matrix = [[mixing[p, i] for i in range(blocks)] for p in range(blocks)]
+
+    def delays(n, d):
+        now = fields[n, d].astype(jnp.float32)
+        before = fields[n, jnp.maximum(d - 1, 0)].astype(jnp.float32)
+        before = jnp.where(d > 0, before, 0.0)
+        return [now] + [
+            jnp.where(lane < k, pltpu.roll(before, k, 1), pltpu.roll(now, k, 1)) for k in (1, 2)
+        ]
+
+    def advances(d):
+        now = gradient[d]
+        after = jnp.where(d < count - 1, gradient[jnp.minimum(d + 1, count - 1)], 0.0)
+        return [now] + [
+            jnp.where(
+                lane >= length - k, pltpu.roll(after, length - k, 1), pltpu.roll(now, length - k, 1)
+            )
+            for k in (1, 2)
+        ]
+
+    def conv(taps, shifted):
+        return taps[0] * shifted[0] + taps[1] * shifted[1] + taps[2] * shifted[2]
+
+    def each_chunk(body):
+        @pl.loop(0, blocks)
+        def _(i):
+            for q in range(per_block):
+                rows = pl.ds(pl.multiple_of(i * share, share), share)
+                body(i * per_block + q, rows, slice(q * length, (q + 1) * length))
+
+    def times_table(source, target):
+        tile = min(256, block)
+
+        @pl.loop(0, block // tile)
+        def _(at):
+            columns = pl.ds(pl.multiple_of(at * tile, tile), tile)
+            product = jnp.dot(source[...], cas[:, columns], preferred_element_type=jnp.float32)
+            target[:, columns] = product.astype(target.dtype)
+
+    def mix(of_values):
+        group = 16
+
+        @pl.loop(0, batch)
+        def _(kt):
+            for inside in range(0, freqs, LANES):
+                columns = pl.ds(pl.multiple_of(kt * freqs + inside, LANES), LANES)
+                part = slice(inside, inside + LANES)
+                per_batch = blocks // batch
+                factor = [
+                    factors[i // per_batch, i % per_batch : i % per_batch + 1, columns]
+                    for i in range(blocks)
+                ]
+                for first in range(0, share, group):
+                    rows = slice(first, first + group)
+                    sums_in = [
+                        wide[i * share + first : i * share + first + group, columns] * factor[i]
+                        for i in range(blocks)
+                    ]
+                    products = []
+                    for p in range(blocks):
+                        mine = matrix[p][0] * sums_in[0]
+                        for i in range(1, blocks):
+                            mine = mine + matrix[p][i] * sums_in[i]
+                        at = slice(p * share + first, p * share + first + group)
+                        if of_values:
+                            spectra[at, columns] = mine
+                        else:
+                            out_spectrum[kt, p, rows, part] = (
+                                spectra[at, columns] * mine
+                            ).astype(out_spectrum.dtype)
+                        products.append(mine * filters[kt, p, rows, part].astype(jnp.float32))
+                    for i in range(blocks):
+                        mine = matrix[0][i] * products[0]
+                        for p in range(1, blocks):
+                            mine = mine + matrix[p][i] * products[p]
+                        weighted[i * share + first : i * share + first + group, columns] = (
+                            mine * factor[i]
+                        ).astype(weighted.dtype)
+
+    wait_in(0)
+
+    @each_chunk
+    def _(d, rows, columns):
+        short_values[rows, columns] = conv(value_taps, delays(0, d)).astype(short_values.dtype)
+
+    times_table(short_values, wide)
+    each_batch(lambda bt: side_copy(1, bt, bt).wait_recv())
+    each_batch(lambda bt: side_copy(0, bt, bt).wait_recv())
+    mix(True)
+    times_table(weighted, filtered)
+
+    wait_in(1)
+    wait_in(2)
+
+    @each_chunk
+    def _(d, rows, columns):
+        shifted = delays(1, d)
+        short_gates = conv(gate_taps, shifted)
+        cot = fields[2, d].astype(jnp.float32)
+        short = short_values[rows, columns].astype(jnp.float32)
+        inner = filtered[rows, columns].astype(jnp.float32) + skip * short
+        out_fields[0, d] = (short_gates * inner).astype(out_fields.dtype)
+        long = (cot * short_gates).astype(grad_long.dtype)
+        grad_long[rows, columns] = long
+        grads = cot * inner
+        gradient[d] = grads
+        for k in range(3):
+            totals[3 + k] += grads * shifted[k]
+        totals[6] += long.astype(jnp.float32) * short
+
+    start_out(0)
+
+    @each_chunk
+    def _(d, rows, columns):
+        out_fields[1, d] = conv(gate_taps, advances(d)).astype(out_fields.dtype)
+
+    start_out(1)
+
+    times_table(grad_long, wide)
+    mix(False)
+    each_batch(lambda bt: side_copy(2, bt, b).start())
+    grad_spectrum[:, batch_rows(b), :] = out_spectrum[b]
+    times_table(weighted, filtered)
+
+    @each_chunk
+    def _(d, rows, columns):
+        grads = skip * grad_long[rows, columns].astype(jnp.float32)
+        grads = grads + filtered[rows, columns].astype(jnp.float32)
+        gradient[d] = grads
+        shifted = delays(0, d)
+        for k in range(3):
+            totals[k] += grads * shifted[k]
+
+    @each_chunk
+    def _(d, rows, columns):
+        out_fields[2, d] = conv(value_taps, advances(d)).astype(out_fields.dtype)
+
+    start_out(2)
+    column = lax.broadcasted_iota(jnp.int32, (share, LANES), 1)
+    line = jnp.zeros((share, LANES), jnp.float32)
+    for k in range(7):
+        line = jnp.where(column == k, jnp.sum(totals[k], axis=1, keepdims=True), line)
+    sums[b] = line
+    each_batch(lambda bt: side_copy(3, bt, b).start())
+
+    for n in range(3):
+        each_other(lambda peer, bt, st: in_copy(n, peer, bt, st, me).wait_send())
+        each_other(lambda peer, bt, st: out_copy(n, peer, bt, st, peer).wait_recv())
+        each_other(lambda peer, bt, st: out_copy(n, peer, bt, st, me).wait_send())
+    for n in range(4):
+        if n >= 2:
+            each_batch(lambda bt: side_copy(n, bt, bt).wait_recv())
+        each_batch(lambda bt: side_copy(n, bt, b).wait_send())
+
+
+def per_device_kernel(
+    values, gates, cotangent, taps_values, taps_gates, skip_gain, twiddle, mixing, spectrum
+):
+    batch, seq = lax.axis_size("batch"), lax.axis_size("seq")
+    count = batch * seq
+    channels, length = values.shape
+    share = channels // count
+    blocks, block = mixing.shape[0], twiddle.shape[1]
+    freqs = block // batch
+    b, s = lax.axis_index("batch"), lax.axis_index("seq")
+    params = jnp.concatenate([taps_values, taps_gates, skip_gain[None], skip_gain[None]], axis=0)
+    params = lax.dynamic_slice_in_dim(params, (s * batch + b) * share, share, 1).T
+    vmem = pl.BlockSpec(memory_space=pltpu.VMEM)
+    smem = pl.BlockSpec(memory_space=pltpu.SMEM)
+    field = jax.ShapeDtypeStruct((channels, length), jnp.bfloat16)
+    rows = blocks * share
+    mixed, grad_values, grad_gates, grad_spectrum, sums = pl.pallas_call(
+        functools.partial(whole_sequences, batch, seq),
+        out_shape=[
+            field, field, field,
+            jax.ShapeDtypeStruct((blocks, channels // seq, freqs), jnp.bfloat16),
+            jax.ShapeDtypeStruct((batch, share, LANES), jnp.float32),
+        ],
+        in_specs=[vmem, vmem, vmem, vmem, vmem, smem, vmem, vmem],
+        out_specs=[vmem] * 5,
+        scratch_shapes=[
+            pltpu.VMEM((3, count, share, length), jnp.bfloat16),
+            pltpu.VMEM((batch, blocks, share, freqs), jnp.bfloat16),
+            pltpu.VMEM((batch, blocks // batch, block), jnp.float32),
+            pltpu.VMEM((rows, block), jnp.bfloat16),
+            pltpu.VMEM((rows, block), jnp.bfloat16),
+            pltpu.VMEM((rows, block), jnp.float32),
+            pltpu.VMEM((rows, block), jnp.bfloat16),
+            pltpu.VMEM((rows, block), jnp.float32),
+            pltpu.VMEM((rows, block), jnp.bfloat16),
+            pltpu.VMEM((count, share, length), jnp.float32),
+            pltpu.VMEM((3, count, share, length), jnp.bfloat16),
+            pltpu.VMEM((batch, blocks, share, freqs), jnp.bfloat16),
+            pltpu.VMEM((7, share, length), jnp.float32),
+            pltpu.SemaphoreType.DMA((3, count)),
+            pltpu.SemaphoreType.DMA((3, count)),
+            pltpu.SemaphoreType.DMA((3, count)),
+            pltpu.SemaphoreType.DMA((3, count)),
+            pltpu.SemaphoreType.DMA((4, batch)),
+            pltpu.SemaphoreType.DMA((4, batch)),
+        ],
+        compiler_params=pltpu.CompilerParams(
+            collective_id=0, has_side_effects=True, vmem_limit_bytes=48 * 2**20
+        ),
+    )(
+        values, gates, cotangent, spectrum.transpose(1, 0, 2), twiddle, mixing, params,
+        cas_table(block),
+    )
+    sums = sums.reshape(channels // seq, LANES).T
+    grad_spectrum = grad_spectrum.transpose(1, 0, 2).astype(jnp.float32)
+    return (
+        mixed, grad_values, grad_gates, grad_spectrum, sums[:3], sums[3:6], sums[6]
+    )
+
+
+def per_device(values, *rest):
+    twiddle, mixing = rest[5], rest[6]
+    batch = lax.axis_size("batch")
+    count = batch * lax.axis_size("seq")
+    channels, length = values.shape
+    block = twiddle.shape[1]
+    fits = (
+        channels % (count * 16) == 0
+        and length % LANES == 0
+        and block % length == 0
+        and block % (batch * LANES) == 0
+        and mixing.shape[0] % batch == 0
+    )
+    return (per_device_kernel if fits else per_device_plain)(values, *rest)
+
+
 def solution(mesh):
     spread = P(None, AXES)
     in_specs = (
@@ -111,5 +447,5 @@
         spread, spread, spread, P("seq", None, "batch"), P(None, "seq"), P(None, "seq"), P("seq")
     )
     return jax.shard_map(
-        per_device_plain, mesh=mesh, in_specs=in_specs, out_specs=out_specs, check_vma=False
-    )
+        per_device, mesh=mesh, in_specs=in_specs, out_specs=out_specs, check_vma=False
+    )

time: 149 us -> 98.8 us (0.66)
  Pallas kernels: 0 us -> 85.9 us
  waiting for transfers between devices: 51.1 us -> 0 us
  blocking collectives: 22.5 us -> 0 us
  local copies, waits for them, and re-layouts: 32.4 us -> 10.9 us
  starting transfers between devices: 17.5 us -> 0 us
  matrix products: 12.5 us -> 0 us
  other arithmetic: 11.6 us -> 0.9 us
    pallas_call x0 -> x1, Pallas kernels: none -> 85.9 us  [per_device_kernel(): pl.pallas_call(functools.partial(whole_sequences, batch, seq), out_shape=...]
    all_to_all x4 -> x0, waiting for transfers between devices: 51.1 us -> none  [the longest x1 26 us: per_device_plain(): lax.all_to_all(stacked, AXES, split_axis=0, concat_axis=0, tiled=True)]
    all_gather x2 -> x0, blocking collectives: 22.5 us -> none  [the longest x1 11.5 us: per_device_plain(): factors = lax.all_gather(twiddle, 'batch', axis=0, tiled=True)]
    all_to_all x4 -> x0, starting transfers between devices: 17.5 us -> none  [the longest x1 5.55 us: per_device_plain(): lax.all_to_all(stacked, AXES, split_axis=0, concat_axis=0, tiled=True)]
    convert_element_type x5 -> x0, local copies, waits for them, and re-layouts: 13.1 us -> none  [the longest x2 4.79 us: back(): return result.reshape(share, -1).astype(jnp.bfloat16).astype(jnp.float32)]
    dot_general x8 -> x0, matrix products: 12.5 us -> none  [the longest x2 5.15 us: back(): jnp.dot(weighted.reshape(-1, block), cas, preferred_element_type=jnp.floa...]
    reduce_sum x2 -> x0, other arithmetic: 6.01 us -> none  [the longest x1 3.76 us: tap_sums(): jnp.sum(gradient * delayed(field, s), axis=1)]
    slice x5 -> x1, local copies, waits for them, and re-layouts: 4.6 us -> 0.58 us  [per_device_kernel(): sums[3:6]]
  transfers between devices with their start and end apart: 4 -> 0, of which waited for: 4 -> 0; matrix products, arithmetic and copies ran while one was open for 14% -> 0% of each run, Pallas kernels for 0% -> 0%
where the time goes in v1:
time: 98.8 us; the launch traced here: 98.4 us
  Pallas kernels  85.9 us (87%)
  local copies, waits for them, and re-layouts  10.9 us (11%)
    pallas_call x1, Pallas kernels, per_device_kernel(): pl.pallas_call(functools.partial(whole_sequences, batch, seq), out_shape=...  85.9 us
    unnamed x16, local copies, waits for them, and re-layouts  9.68 us

profile of v1, /device:TPU:0, one launch (start us, length us, event | category | flops | bytes accessed | tf_op | source)
XLA Modules:
  0.0 98.4 jit_solution(14719895308995487750)
XLA Ops:
  0.6 0.8 fusion.2
  1.5 0.1 copy.33
  1.5 1.1 %copy.35 = bf16[128,8,256]{2,0,1:T(8,128)(2,1)S(1)} copy(bf16[128,8,256]{2,1,0:T(8,128)(2,1)} %param.18) | data formatting | bytes 1048576 | tf_op args[8]
  2.7 0.0 copy-start
  2.7 1.0 %copy-done = bf16[1024,256]{1,0:T(8,128)(2,1)S(1)} copy-done((bf16[1024,256]{1,0:T(8,128)(2,1)S(1)}, bf16[1024,256]{1,0:T(8,128)(2,1)}, u32[]{:S(2)}) %copy-start) | copy-done | bytes 524312
  3.7 0.0 copy-start.1
  3.7 1.0 %copy-done.1 = bf16[1024,256]{1,0:T(8,128)(2,1)S(1)} copy-done((bf16[1024,256]{1,0:T(8,128)(2,1)S(1)}, bf16[1024,256]{1,0:T(8,128)(2,1)}, u32[]{:S(2)}) %copy-start.1) | copy-done | bytes 524312
  4.8 0.0 copy-start.2
  4.8 1.0 %copy-done.2 = bf16[1024,256]{1,0:T(8,128)(2,1)S(1)} copy-done((bf16[1024,256]{1,0:T(8,128)(2,1)S(1)}, bf16[1024,256]{1,0:T(8,128)(2,1)}, u32[]{:S(2)}) %copy-start.2) | copy-done | bytes 524312
  5.8 0.0 copy-start.3
  5.8 0.7 copy-done.3
  6.5 0.0 copy-start.4
  6.5 0.7 copy-done.4
  7.2 85.9 %shard_map.153 = (bf16[1024,256]{1,0:T(8,128)(2,1)S(1)}, bf16[1024,256]{1,0:T(8,128)(2,1)S(1)}, bf16[1024,256]{1,0:T(8,128)(2,1)S(1)}, bf16[8,128,256]{2,1,0:T(8,128)(2,1)S(1)}, f32[4,32,128]{2,1,0:T(8,128)S(1)}) custom-call(bf16[1024,256]{1,0:T(8,128)(2,1)S(1)} %copy-done, bf16[1024,256]{1,0:T(8,128)(2,1)S(1)} %copy-done.1, ...), custom_call_target="tpu_custom_call" | custom-call | tf_op jit(solution)/shard_map/pallas_call | solution.py:381
  93.1 0.1 copy.31
  93.2 0.5 slice_bitcast_fusion
  93.7 0.6 fusion.3
  94.3 0.1 convert_bitcast_fusion
  94.4 1.6 %copy.32 = f32[128,8,256]{2,1,0:T(8,128)} copy(f32[128,8,256]{2,0,1:T(8,128)S(1)} %convert_bitcast_fusion) | data formatting | bytes 2097152
  96.0 0.8 copy.39
  96.8 0.8 copy.40
  97.6 0.8 copy.41
Async XLA Ops:
  2.7 1.0 %copy-start = (bf16[1024,256]{1,0:T(8,128)(2,1)S(1)}, bf16[1024,256]{1,0:T(8,128)(2,1)}, u32[]{:S(2)}) copy-start(bf16[1024,256]{1,0:T(8,128)(2,1)} %values.1) | copy-start | bytes 1572868
  3.7 1.0 %copy-start.1 = (bf16[1024,256]{1,0:T(8,128)(2,1)S(1)}, bf16[1024,256]{1,0:T(8,128)(2,1)}, u32[]{:S(2)}) copy-start(bf16[1024,256]{1,0:T(8,128)(2,1)} %gates.1) | copy-start | bytes 1572868
  4.8 1.0 %copy-start.2 = (bf16[1024,256]{1,0:T(8,128)(2,1)S(1)}, bf16[1024,256]{1,0:T(8,128)(2,1)}, u32[]{:S(2)}) copy-start(bf16[1024,256]{1,0:T(8,128)(2,1)} %cotangent.1) | copy-start | bytes 1572868
  5.8 0.7 copy-start.3
  6.5 0.7 copy-start.4

commit v2 on v1

--- a/solution.py
+++ b/solution.py
@@ -111,11 +111,13 @@
 
 def whole_sequences(
     batch, seq,
-    values, gates, cotangent, spectrum, twiddle, mixing, params, cas,
-    mixed, grad_values, grad_gates, grad_spectrum, sums,
-    fields, filters, factors, short_values, grad_long, wide, weighted, spectra, filtered, gradient,
-    out_fields, out_spectrum, totals,
-    in_send, in_recv, out_send, out_recv, side_send, side_recv,
+    values, gates_in, cotangent_in, spectrum, twiddle, mixing, params, cas_in,
+    mixed, grad_values, grad_gates, grad_spectrum, sums, gate_sums,
+    gates, cotangent, cas, fields, filters, factors, short_values, grad_long, wide, weighted,
+    spectra, filtered, gradient, out_fields, out_spectrum, totals,
+    short_gates, long_here, inner_here, gates_gradient, before, after, rims, line, parts, batch_parts,
+    in_send, in_recv, out_send, out_recv, side_send, side_recv, rim_send, rim_recv,
+    part_send, part_recv, local,
 ):
     b, s = lax.axis_index("batch"), lax.axis_index("seq")
     count = batch * seq
@@ -152,7 +154,7 @@
 
     def in_copy(n, peer, bt, st, slot):
         return pltpu.make_async_remote_copy(
-            src_ref=(values, gates, cotangent)[n].at[rows_of(bt, st), :],
+            src_ref=(values, long_here)[n].at[rows_of(bt, st), :],
             dst_ref=fields.at[n, me],
             send_sem=in_send.at[n, peer],
             recv_sem=in_recv.at[n, slot],
@@ -163,7 +165,7 @@
     def out_copy(n, peer, bt, st, slot):
         return pltpu.make_async_remote_copy(
             src_ref=out_fields.at[n, peer],
-            dst_ref=(mixed, grad_gates, grad_values)[n].at[rows_of(b, s), :],
+            dst_ref=(inner_here, grad_values)[n].at[rows_of(b, s), :],
             send_sem=out_send.at[n, peer],
             recv_sem=out_recv.at[n, slot],
             device_id=(bt, st),
@@ -171,8 +173,12 @@
         )
 
     def side_copy(n, bt, slot):
-        source = (spectrum.at[:, batch_rows(bt), :], twiddle, out_spectrum.at[bt], sums.at[b])[n]
-        target = (filters.at[b], factors.at[b], grad_spectrum.at[:, batch_rows(b), :], sums.at[b])[n]
+        source = (
+            spectrum.at[:, batch_rows(bt), :], twiddle, out_spectrum.at[bt], sums.at[b], batch_parts.at[b]
+        )[n]
+        target = (
+            filters.at[b], factors.at[b], grad_spectrum.at[:, batch_rows(b), :], sums.at[b], batch_parts.at[b]
+        )[n]
         return pltpu.make_async_remote_copy(
             src_ref=source,
             dst_ref=target,
@@ -182,6 +188,33 @@
             device_id_type=MESH,
         )
 
+    def rim_copy(n):
+        peer = lax.rem(me + (1, count - 1)[n], count)
+        return pltpu.make_async_remote_copy(
+            src_ref=rims.at[n],
+            dst_ref=rims.at[2 + n],
+            send_sem=rim_send.at[n],
+            recv_sem=rim_recv.at[n],
+            device_id=(lax.div(peer, seq), lax.rem(peer, seq)),
+            device_id_type=MESH,
+        )
+
+    width = values.shape[0] // seq
+
+    def part_copy(st, slot):
+        return pltpu.make_async_remote_copy(
+            src_ref=parts.at[0, st],
+            dst_ref=parts.at[1, s],
+            send_sem=part_send.at[st],
+            recv_sem=part_recv.at[slot],
+            device_id=(b, st),
+            device_id_type=MESH,
+        )
+
+    def each_seq(body):
+        for step in range(1, seq):
+            body(lax.rem(s + step, seq))
+
     def start_in(n):
         each_other(lambda peer, bt, st: in_copy(n, peer, bt, st, me).start())
 
@@ -190,42 +223,61 @@
 
     def start_out(n):
         each_other(lambda peer, bt, st: out_copy(n, peer, bt, st, me).start())
-        (mixed, grad_gates, grad_values)[n][rows_of(b, s), :] = out_fields[n, me]
-
+        (inner_here, grad_values)[n][rows_of(b, s), :] = out_fields[n, me]
+
+    load_gates = pltpu.make_async_copy(gates_in, gates, local.at[0])
+    load_cotangent = pltpu.make_async_copy(cotangent_in, cotangent, local.at[1])
+    load_cas = pltpu.make_async_copy(cas_in, cas, local.at[2])
+    load_values = pltpu.make_async_copy(values.at[rows_of(b, s), :], fields.at[0, me], local.at[3])
+    load_filters = pltpu.make_async_copy(
+        spectrum.at[:, batch_rows(b), :], filters.at[b], local.at[4]
+    )
+    load_gates.start()
+    load_cotangent.start()
     start_in(0)
     each_batch(lambda bt: side_copy(1, bt, b).start())
     each_batch(lambda bt: side_copy(0, bt, b).start())
-    start_in(1)
-    start_in(2)
-    for n, source in enumerate((values, gates, cotangent)):
-        fields[n, me] = source[rows_of(b, s), :]
-    filters[b] = spectrum[:, batch_rows(b), :]
+    load_values.start()
+    load_cas.start()
+    load_filters.start()
     factors[b] = twiddle[...]
     totals[...] = jnp.zeros_like(totals)
 
     lane = lax.broadcasted_iota(jnp.int32, (share, length), 1)
-    value_taps = [params[:, n : n + 1] for n in range(3)]
-    gate_taps = [params[:, n : n + 1] for n in range(3, 6)]
-    skip = params[:, 6:7]
+    mine_rows = rows_of(b, s)
+    value_taps = [params[mine_rows, n : n + 1] for n in range(3)]
+    skip = params[mine_rows, 6:7]
     matrix = [[mixing[p, i] for i in range(blocks)] for p in range(blocks)]
 
-    def delays(n, d):
-        now = fields[n, d].astype(jnp.float32)
-        before = fields[n, jnp.maximum(d - 1, 0)].astype(jnp.float32)
-        before = jnp.where(d > 0, before, 0.0)
+    def delayed_by(now, earlier):
         return [now] + [
-            jnp.where(lane < k, pltpu.roll(before, k, 1), pltpu.roll(now, k, 1)) for k in (1, 2)
+            jnp.where(lane < k, pltpu.roll(earlier, k, 1), pltpu.roll(now, k, 1)) for k in (1, 2)
         ]
 
-    def advances(d):
-        now = gradient[d]
-        after = jnp.where(d < count - 1, gradient[jnp.minimum(d + 1, count - 1)], 0.0)
+    def advanced_by(now, later):
         return [now] + [
             jnp.where(
-                lane >= length - k, pltpu.roll(after, length - k, 1), pltpu.roll(now, length - k, 1)
+                lane >= length - k, pltpu.roll(later, length - k, 1), pltpu.roll(now, length - k, 1)
             )
             for k in (1, 2)
         ]
+
+    def delays(d):
+        now = fields[0, d].astype(jnp.float32)
+        earlier = fields[0, jnp.maximum(d - 1, 0)].astype(jnp.float32)
+        return delayed_by(now, jnp.where(d > 0, earlier, 0.0))
+
+    def advances(d):
+        later = jnp.where(d < count - 1, gradient[jnp.minimum(d + 1, count - 1)], 0.0)
+        return advanced_by(gradient[d], later)
+
+    def gate_taps(rows):
+        return [params[rows, n : n + 1] for n in range(3, 6)]
+
+    def each_group(body):
+        @pl.loop(0, count)
+        def _(g):
+            body(pl.ds(pl.multiple_of(g * share, share), share))
 
     def conv(taps, shifted):
         return taps[0] * shifted[0] + taps[1] * shifted[1] + taps[2] * shifted[2]
@@ -286,44 +338,55 @@
                             mine * factor[i]
                         ).astype(weighted.dtype)
 
+    load_gates.wait()
+    last = gates[:, length - LANES :].astype(jnp.float32).T
+    rims[0] = last[LANES - 8 :, :]
+    rim_copy(0).start()
+    load_cotangent.wait()
+    rim_copy(0).wait_recv()
+    came = jnp.where(me > 0, rims[2], 0.0)
+    padded = jnp.concatenate([jnp.zeros((LANES - 8, came.shape[1]), jnp.float32), came], axis=0)
+    before[...] = jnp.zeros_like(before)
+    before[:, length - LANES :] = padded.T
+
+    @each_group
+    def _(rows):
+        shifted = delayed_by(gates[rows, :].astype(jnp.float32), before[rows, :])
+        short = conv(gate_taps(rows), shifted)
+        short_gates[rows, :] = short
+        long_here[rows, :] = (cotangent[rows, :].astype(jnp.float32) * short).astype(long_here.dtype)
+
+    start_in(1)
+    fields[1, me] = long_here[rows_of(b, s), :]
+
+    load_values.wait()
     wait_in(0)
 
     @each_chunk
     def _(d, rows, columns):
-        short_values[rows, columns] = conv(value_taps, delays(0, d)).astype(short_values.dtype)
-
+        short_values[rows, columns] = conv(value_taps, delays(d)).astype(short_values.dtype)
+
+    load_cas.wait()
     times_table(short_values, wide)
+    load_filters.wait()
     each_batch(lambda bt: side_copy(1, bt, bt).wait_recv())
     each_batch(lambda bt: side_copy(0, bt, bt).wait_recv())
     mix(True)
     times_table(weighted, filtered)
 
-    wait_in(1)
-    wait_in(2)
-
     @each_chunk
     def _(d, rows, columns):
-        shifted = delays(1, d)
-        short_gates = conv(gate_taps, shifted)
-        cot = fields[2, d].astype(jnp.float32)
         short = short_values[rows, columns].astype(jnp.float32)
         inner = filtered[rows, columns].astype(jnp.float32) + skip * short
-        out_fields[0, d] = (short_gates * inner).astype(out_fields.dtype)
-        long = (cot * short_gates).astype(grad_long.dtype)
-        grad_long[rows, columns] = long
-        grads = cot * inner
-        gradient[d] = grads
-        for k in range(3):
-            totals[3 + k] += grads * shifted[k]
-        totals[6] += long.astype(jnp.float32) * short
+        out_fields[0, d] = inner.astype(out_fields.dtype)
 
     start_out(0)
+
+    wait_in(1)
 
     @each_chunk
     def _(d, rows, columns):
-        out_fields[1, d] = conv(gate_taps, advances(d)).astype(out_fields.dtype)
-
-    start_out(1)
+        grad_long[rows, columns] = fields[1, d]
 
     times_table(grad_long, wide)
     mix(False)
@@ -334,32 +397,86 @@
     @each_chunk
     def _(d, rows, columns):
         grads = skip * grad_long[rows, columns].astype(jnp.float32)
-        grads = grads + filtered[rows, columns].astype(jnp.float32)
-        gradient[d] = grads
-        shifted = delays(0, d)
+        gradient[d] = grads + filtered[rows, columns].astype(jnp.float32)
+
+    @each_chunk
+    def _(d, rows, columns):
+        out_fields[1, d] = conv(value_taps, advances(d)).astype(out_fields.dtype)
+
+    start_out(1)
+
+    @each_chunk
+    def _(d, rows, columns):
+        shifted = delays(d)
+        grads = gradient[d]
         for k in range(3):
             totals[k] += grads * shifted[k]
-
-    @each_chunk
-    def _(d, rows, columns):
-        out_fields[2, d] = conv(value_taps, advances(d)).astype(out_fields.dtype)
-
-    start_out(2)
+        totals[3] += grad_long[rows, columns].astype(jnp.float32) * short_values[
+            rows, columns
+        ].astype(jnp.float32)
+
     column = lax.broadcasted_iota(jnp.int32, (share, LANES), 1)
-    line = jnp.zeros((share, LANES), jnp.float32)
-    for k in range(7):
-        line = jnp.where(column == k, jnp.sum(totals[k], axis=1, keepdims=True), line)
-    sums[b] = line
+
+    def in_columns(columns):
+        result = jnp.zeros((share, LANES), jnp.float32)
+        for k, value in enumerate(columns):
+            result = jnp.where(column == k, jnp.sum(value, axis=1, keepdims=True), result)
+        return result
+
+    sums[b] = in_columns([totals[k] for k in range(4)])
     each_batch(lambda bt: side_copy(3, bt, b).start())
 
-    for n in range(3):
+    each_other(lambda peer, bt, st: out_copy(0, peer, bt, st, peer).wait_recv())
+
+    @each_group
+    def _(rows):
+        inner = inner_here[rows, :].astype(jnp.float32)
+        mixed[rows, :] = (short_gates[rows, :] * inner).astype(mixed.dtype)
+        grads = cotangent[rows, :].astype(jnp.float32) * inner
+        gates_gradient[rows, :] = grads
+        shifted = delayed_by(gates[rows, :].astype(jnp.float32), before[rows, :])
+        line[rows, :] = in_columns([grads * shifted[k] for k in range(3)])
+
+    rims[1] = gates_gradient[:, :LANES].T[:8, :]
+    rim_copy(1).start()
+    turned = line[...].T[:8, :]
+    for st in range(seq):
+        parts[0, st] = turned[:, st * width : (st + 1) * width]
+    each_seq(lambda st: part_copy(st, s).start())
+    parts[1, s] = parts[0, s]
+    rim_copy(1).wait_recv()
+    came = jnp.where(me < count - 1, rims[3], 0.0)
+    padded = jnp.concatenate([came, jnp.zeros((LANES - 8, came.shape[1]), jnp.float32)], axis=0)
+    after[...] = jnp.zeros_like(after)
+    after[:, :LANES] = padded.T
+
+    @each_group
+    def _(rows):
+        shifted = advanced_by(gates_gradient[rows, :], after[rows, :])
+        grad_gates[rows, :] = conv(gate_taps(rows), shifted).astype(grad_gates.dtype)
+
+    each_seq(lambda st: part_copy(st, st).wait_recv())
+    total = parts[1, 0]
+    for st in range(1, seq):
+        total = total + parts[1, st]
+    batch_parts[b] = total
+    each_batch(lambda bt: side_copy(4, bt, b).start())
+    each_batch(lambda bt: side_copy(4, bt, bt).wait_recv())
+    total = batch_parts[0]
+    for bt in range(1, batch):
+        total = total + batch_parts[bt]
+    gate_sums[...] = total
+
+    each_seq(lambda st: part_copy(st, s).wait_send())
+    for n in range(2):
+        rim_copy(n).wait_send()
         each_other(lambda peer, bt, st: in_copy(n, peer, bt, st, me).wait_send())
-        each_other(lambda peer, bt, st: out_copy(n, peer, bt, st, peer).wait_recv())
         each_other(lambda peer, bt, st: out_copy(n, peer, bt, st, me).wait_send())
-    for n in range(4):
-        if n >= 2:
+    for n in range(5):
+        if n in (2, 3):
             each_batch(lambda bt: side_copy(n, bt, bt).wait_recv())
         each_batch(lambda bt: side_copy(n, bt, b).wait_send())
+    each_other(lambda peer, bt, st: out_copy(1, peer, bt, st, peer).wait_recv())
 
 
 def per_device_kernel(
@@ -371,24 +488,27 @@
     share = channels // count
     blocks, block = mixing.shape[0], twiddle.shape[1]
     freqs = block // batch
-    b, s = lax.axis_index("batch"), lax.axis_index("seq")
-    params = jnp.concatenate([taps_values, taps_gates, skip_gain[None], skip_gain[None]], axis=0)
-    params = lax.dynamic_slice_in_dim(params, (s * batch + b) * share, share, 1).T
+    params = jnp.concatenate([taps_values, taps_gates, skip_gain[None], skip_gain[None]], axis=0).T
     vmem = pl.BlockSpec(memory_space=pltpu.VMEM)
+    hbm = pl.BlockSpec(memory_space=pl.ANY)
     smem = pl.BlockSpec(memory_space=pltpu.SMEM)
     field = jax.ShapeDtypeStruct((channels, length), jnp.bfloat16)
     rows = blocks * share
-    mixed, grad_values, grad_gates, grad_spectrum, sums = pl.pallas_call(
+    mixed, grad_values, grad_gates, grad_spectrum, sums, gate_sums = pl.pallas_call(
         functools.partial(whole_sequences, batch, seq),
         out_shape=[
             field, field, field,
             jax.ShapeDtypeStruct((blocks, channels // seq, freqs), jnp.bfloat16),
             jax.ShapeDtypeStruct((batch, share, LANES), jnp.float32),
+            jax.ShapeDtypeStruct((8, channels // seq), jnp.float32),
         ],
-        in_specs=[vmem, vmem, vmem, vmem, vmem, smem, vmem, vmem],
-        out_specs=[vmem] * 5,
+        in_specs=[hbm, hbm, hbm, hbm, vmem, smem, vmem, hbm],
+        out_specs=[vmem] * 6,
         scratch_shapes=[
-            pltpu.VMEM((3, count, share, length), jnp.bfloat16),
+            pltpu.VMEM((channels, length), jnp.bfloat16),
+            pltpu.VMEM((channels, length), jnp.bfloat16),
+            pltpu.VMEM((block, block), jnp.bfloat16),
+            pltpu.VMEM((2, count, share, length), jnp.bfloat16),
             pltpu.VMEM((batch, blocks, share, freqs), jnp.bfloat16),
             pltpu.VMEM((batch, blocks // batch, block), jnp.float32),
             pltpu.VMEM((rows, block), jnp.bfloat16),
@@ -398,18 +518,33 @@
             pltpu.VMEM((rows, block), jnp.float32),
             pltpu.VMEM((rows, block), jnp.bfloat16),
             pltpu.VMEM((count, share, length), jnp.float32),
-            pltpu.VMEM((3, count, share, length), jnp.bfloat16),
+            pltpu.VMEM((2, count, share, length), jnp.bfloat16),
             pltpu.VMEM((batch, blocks, share, freqs), jnp.bfloat16),
-            pltpu.VMEM((7, share, length), jnp.float32),
-            pltpu.SemaphoreType.DMA((3, count)),
-            pltpu.SemaphoreType.DMA((3, count)),
-            pltpu.SemaphoreType.DMA((3, count)),
-            pltpu.SemaphoreType.DMA((3, count)),
-            pltpu.SemaphoreType.DMA((4, batch)),
-            pltpu.SemaphoreType.DMA((4, batch)),
+            pltpu.VMEM((4, share, length), jnp.float32),
+            pltpu.VMEM((channels, length), jnp.float32),
+            pltpu.VMEM((channels, length), jnp.bfloat16),
+            pltpu.VMEM((channels, length), jnp.bfloat16),
+            pltpu.VMEM((channels, length), jnp.float32),
+            pltpu.VMEM((channels, length), jnp.float32),
+            pltpu.VMEM((channels, length), jnp.float32),
+            pltpu.VMEM((4, 8, channels), jnp.float32),
+            pltpu.VMEM((channels, LANES), jnp.float32),
+            pltpu.VMEM((2, seq, 8, channels // seq), jnp.float32),
+            pltpu.VMEM((batch, 8, channels // seq), jnp.float32),
+            pltpu.SemaphoreType.DMA((2, count)),
+            pltpu.SemaphoreType.DMA((2, count)),
+            pltpu.SemaphoreType.DMA((2, count)),
+            pltpu.SemaphoreType.DMA((2, count)),
+            pltpu.SemaphoreType.DMA((5, batch)),
+            pltpu.SemaphoreType.DMA((5, batch)),
+            pltpu.SemaphoreType.DMA((2,)),
+            pltpu.SemaphoreType.DMA((2,)),
+            pltpu.SemaphoreType.DMA((seq,)),
+            pltpu.SemaphoreType.DMA((seq,)),
+            pltpu.SemaphoreType.DMA((5,)),
         ],
         compiler_params=pltpu.CompilerParams(
-            collective_id=0, has_side_effects=True, vmem_limit_bytes=48 * 2**20
+            collective_id=0, has_side_effects=True, vmem_limit_bytes=56 * 2**20
         ),
     )(
         values, gates, cotangent, spectrum.transpose(1, 0, 2), twiddle, mixing, params,
@@ -418,7 +553,7 @@
     sums = sums.reshape(channels // seq, LANES).T
     grad_spectrum = grad_spectrum.transpose(1, 0, 2).astype(jnp.float32)
     return (
-        mixed, grad_values, grad_gates, grad_spectrum, sums[:3], sums[3:6], sums[6]
+        mixed, grad_values, grad_gates, grad_spectrum, sums[:3], gate_sums[:3], sums[3]
     )
 
 
@@ -431,6 +566,7 @@
     fits = (
         channels % (count * 16) == 0
         and length % LANES == 0
+        and channels % (lax.axis_size("seq") * LANES) == 0
         and block % length == 0
         and block % (batch * LANES) == 0
         and mixing.shape[0] % batch == 0

time: 98.8 us -> 86 us (0.87)
  Pallas kernels: 85.9 us -> 72.7 us
  other arithmetic: 0.9 us -> 1.97 us
    pallas_call x1, Pallas kernels: 85.9 us -> 72.7 us  [per_device_kernel(): pl.pallas_call(functools.partial(whole_sequences, batch, seq), out_shape=...]
    unnamed x16 -> x11, local copies, waits for them, and re-layouts: 9.68 us -> 5.91 us
    slice x1 -> x2, local copies, waits for them, and re-layouts: 0.58 us -> 1.9 us  [the longest x1 1.32 us: per_device_kernel(): gate_sums[:3]]
    convert_element_type x1, other arithmetic: 0.09 us -> 1.18 us  [per_device_kernel(): grad_spectrum = grad_spectrum.transpose(1, 0, 2).astype(jnp.float32)]
    concatenate x0 -> x1, local copies, waits for them, and re-layouts: none -> 1 us  [per_device_kernel(): jnp.concatenate([taps_values, taps_gates, skip_gain[None], skip_gain[None...]
where the time goes in v2:
time: 86 us; the launch traced here: 85.6 us
  Pallas kernels  72.7 us (85%)
  local copies, waits for them, and re-layouts  10.3 us (12%)
  other arithmetic  1.97 us (2%)
    pallas_call x1, Pallas kernels, per_device_kernel(): pl.pallas_call(functools.partial(whole_sequences, batch, seq), out_shape=...  72.7 us
    unnamed x11, local copies, waits for them, and re-layouts  5.91 us

profile of v2, /device:TPU:0, one launch (start us, length us, event | category | flops | bytes accessed | tf_op | source)
XLA Modules:
  0.0 85.6 jit_solution(9878496896564831801)
XLA Ops:
  0.6 0.8 pad_maximum_fusion
  1.4 1.0 %copy.30 = f32[8,1024]{0,1:T(8,128)} copy(f32[8,1024]{1,0:T(8,128)S(1)} %pad_maximum_fusion) | data formatting | bytes 65536 | tf_op jit(solution)/shard_map/concatenate | solution.py:491
  2.4 1.9 %copy.34 = bf16[128,8,256]{2,0,1:T(8,128)(2,1)} copy(bf16[128,8,256]{2,1,0:T(8,128)(2,1)} %param.18) | data formatting | bytes 1048576 | tf_op args[8]
  4.4 72.7 %shard_map.153 = (bf16[1024,256]{1,0:T(8,128)(2,1)}, bf16[1024,256]{1,0:T(8,128)(2,1)}, bf16[1024,256]{1,0:T(8,128)(2,1)}, bf16[8,128,256]{2,1,0:T(8,128)(2,1)},...) custom-call(bf16[1024,256]{1,0:T(8,128)(2,1)} %values.1, bf16[1024,256]{1,0:T(8,128)(2,1)} %gates_in.1, ...), custom_call_target="tpu_custom_call" | custom-call | tf_op jit(solution)/shard_map/pallas_call | solution.py:497
  77.1 0.0 copy-start.2
  77.1 1.3 %slice.10 = f32[3,128]{1,0:T(4,128)} slice(f32[8,128]{1,0:T(8,128)} %get-tuple-element.18), slice={[0:3], [0:128]} | slice | bytes 3072 | tf_op jit(solution)/shard_map/slice | solution.py:556
  78.4 0.9 %copy.31 = f32[128,128]{0,1:T(8,128)S(1)} copy(f32[128,128]{1,0:T(8,128)} %bitcast.15) | data formatting | bytes 131072 | tf_op jit(solution)/shard_map/reshape | solution.py:553
  79.4 0.5 slice_bitcast_fusion
  79.9 0.6 slice.12
  80.5 0.0 copy-start.1
  80.5 1.2 %convert_bitcast_fusion = f32[128,8,256]{2,0,1:T(8,128)S(1)} fusion(bf16[8,128,256]{2,1,0:T(8,128)(2,1)} %get-tuple-element.16), kind=kLoop, calls=%fused_computation | loop fusion | flops 262144 | bytes 1572864 | tf_op jit(solution)/shard_map/convert_element_type | solution.py:554
  81.7 0.0 copy-start
  81.7 1.6 %copy.32 = f32[128,8,256]{2,1,0:T(8,128)} copy(f32[128,8,256]{2,0,1:T(8,128)S(1)} %convert_bitcast_fusion) | data formatting | bytes 2097152
  83.2 0.0 copy-done.2
  83.3 0.8 copy.38
  84.0 0.0 copy-done.1
  84.0 0.8 copy.39
  84.8 0.0 copy-done
  84.8 0.8 copy.40
Async XLA Ops:
  77.1 6.1 %copy-start.2 = (bf16[1024,256]{1,0:T(8,128)(2,1)S(1)}, bf16[1024,256]{1,0:T(8,128)(2,1)}, u32[]{:S(2)}) copy-start(bf16[1024,256]{1,0:T(8,128)(2,1)} %get-tuple-element.47) | copy-start | bytes 1572868
  80.5 3.6 %copy-start.1 = (bf16[1024,256]{1,0:T(8,128)(2,1)S(1)}, bf16[1024,256]{1,0:T(8,128)(2,1)}, u32[]{:S(2)}) copy-start(bf16[1024,256]{1,0:T(8,128)(2,1)} %get-tuple-element.48) | copy-start | bytes 1572868
  81.7 3.2 %copy-start = (bf16[1024,256]{1,0:T(8,128)(2,1)S(1)}, bf16[1024,256]{1,0:T(8,128)(2,1)}, u32[]{:S(2)}) copy-start(bf16[1024,256]{1,0:T(8,128)(2,1)} %get-tuple-element.49) | copy-start | bytes 1572868

commit v3 on v2

--- a/solution.py
+++ b/solution.py
@@ -111,9 +111,10 @@
 
 def whole_sequences(
     batch, seq,
-    values, gates_in, cotangent_in, spectrum, twiddle, mixing, params, cas_in,
-    mixed, grad_values, grad_gates, grad_spectrum, sums, gate_sums,
-    gates, cotangent, cas, fields, filters, factors, short_values, grad_long, wide, weighted,
+    values, gates_in, cotangent_in, spectrum, twiddle, mixing, value_taps_in, gate_taps_in, skip_in, cas_in,
+    mixed, grad_values, grad_gates, grad_spectrum, value_sums, gate_sums, skip_sums,
+    gates, cotangent, cas, params, turned_params, filters_landed, unpacked, spectrum_landed, sums,
+    fields, filters, factors, short_values, grad_long, wide, weighted,
     spectra, filtered, gradient, out_fields, out_spectrum, totals,
     short_gates, long_here, inner_here, gates_gradient, before, after, rims, line, parts, batch_parts,
     in_send, in_recv, out_send, out_recv, side_send, side_recv, rim_send, rim_recv,
@@ -147,9 +148,29 @@
         for step in range(1, batch):
             body(lax.rem(b + step, batch))
 
+    load_gates = pltpu.make_async_copy(gates_in, gates, local.at[0])
+    load_cotangent = pltpu.make_async_copy(cotangent_in, cotangent, local.at[1])
+    load_cas = pltpu.make_async_copy(cas_in, cas, local.at[2])
+    load_values = pltpu.make_async_copy(values.at[rows_of(b, s), :], fields.at[0, me], local.at[3])
+    load_filters = pltpu.make_async_copy(
+        spectrum.at[batch_rows(b)], filters_landed.at[b], local.at[4]
+    )
+
     barrier = pltpu.get_barrier_semaphore()
     each_other(lambda peer, bt, st: pl.semaphore_signal(
         barrier, inc=1, device_id=(bt, st), device_id_type=MESH))
+    load_gates.start()
+    load_cotangent.start()
+    load_values.start()
+    load_cas.start()
+    load_filters.start()
+    turned_params[...] = jnp.zeros_like(turned_params)
+    turned_params[0:3, :] = value_taps_in[...]
+    turned_params[3:6, :] = gate_taps_in[...]
+    turned_params[6:7, :] = skip_in[...]
+    params[...] = turned_params[...].T
+    load_gates.wait()
+    rims[0] = gates[:, length - LANES :].astype(jnp.float32).T[LANES - 8 :, :]
     pl.semaphore_wait(barrier, count - 1)
 
     def in_copy(n, peer, bt, st, slot):
@@ -174,10 +195,10 @@
 
     def side_copy(n, bt, slot):
         source = (
-            spectrum.at[:, batch_rows(bt), :], twiddle, out_spectrum.at[bt], sums.at[b], batch_parts.at[b]
+            spectrum.at[batch_rows(bt)], twiddle, out_spectrum.at[bt], sums.at[b], batch_parts.at[b]
         )[n]
         target = (
-            filters.at[b], factors.at[b], grad_spectrum.at[:, batch_rows(b), :], sums.at[b], batch_parts.at[b]
+            filters_landed.at[b], factors.at[b], spectrum_landed.at[:, batch_rows(b), :], sums.at[b], batch_parts.at[b]
         )[n]
         return pltpu.make_async_remote_copy(
             src_ref=source,
@@ -225,21 +246,10 @@
         each_other(lambda peer, bt, st: out_copy(n, peer, bt, st, me).start())
         (inner_here, grad_values)[n][rows_of(b, s), :] = out_fields[n, me]
 
-    load_gates = pltpu.make_async_copy(gates_in, gates, local.at[0])
-    load_cotangent = pltpu.make_async_copy(cotangent_in, cotangent, local.at[1])
-    load_cas = pltpu.make_async_copy(cas_in, cas, local.at[2])
-    load_values = pltpu.make_async_copy(values.at[rows_of(b, s), :], fields.at[0, me], local.at[3])
-    load_filters = pltpu.make_async_copy(
-        spectrum.at[:, batch_rows(b), :], filters.at[b], local.at[4]
-    )
-    load_gates.start()
-    load_cotangent.start()
+    rim_copy(0).start()
     start_in(0)
     each_batch(lambda bt: side_copy(1, bt, b).start())
     each_batch(lambda bt: side_copy(0, bt, b).start())
-    load_values.start()
-    load_cas.start()
-    load_filters.start()
     factors[b] = twiddle[...]
     totals[...] = jnp.zeros_like(totals)
 
@@ -329,7 +339,7 @@
                             out_spectrum[kt, p, rows, part] = (
                                 spectra[at, columns] * mine
                             ).astype(out_spectrum.dtype)
-                        products.append(mine * filters[kt, p, rows, part].astype(jnp.float32))
+                        products.append(mine * filters[kt, p, rows, part])
                     for i in range(blocks):
                         mine = matrix[0][i] * products[0]
                         for p in range(1, blocks):
@@ -338,10 +348,6 @@
                             mine * factor[i]
                         ).astype(weighted.dtype)
 
-    load_gates.wait()
-    last = gates[:, length - LANES :].astype(jnp.float32).T
-    rims[0] = last[LANES - 8 :, :]
-    rim_copy(0).start()
     load_cotangent.wait()
     rim_copy(0).wait_recv()
     came = jnp.where(me > 0, rims[2], 0.0)
@@ -359,6 +365,17 @@
     start_in(1)
     fields[1, me] = long_here[rows_of(b, s), :]
 
+    load_filters.wait()
+    each_batch(lambda bt: side_copy(1, bt, bt).wait_recv())
+    each_batch(lambda bt: side_copy(0, bt, bt).wait_recv())
+    for bt in range(batch):
+        flat = filters_landed[bt].astype(jnp.float32).reshape(share * blocks, freqs)
+        for half in range(freqs // LANES):
+            lanes = slice(half * LANES, (half + 1) * LANES)
+            unpacked[half] = flat[:, lanes]
+            for p in range(blocks):
+                filters[bt, p, :, lanes] = unpacked[half, pl.ds(p, share, stride=blocks), :]
+
     load_values.wait()
     wait_in(0)
 
@@ -368,9 +385,6 @@
 
     load_cas.wait()
     times_table(short_values, wide)
-    load_filters.wait()
-    each_batch(lambda bt: side_copy(1, bt, bt).wait_recv())
-    each_batch(lambda bt: side_copy(0, bt, bt).wait_recv())
     mix(True)
     times_table(weighted, filtered)
 
@@ -391,7 +405,7 @@
     times_table(grad_long, wide)
     mix(False)
     each_batch(lambda bt: side_copy(2, bt, b).start())
-    grad_spectrum[:, batch_rows(b), :] = out_spectrum[b]
+    spectrum_landed[:, batch_rows(b), :] = out_spectrum[b]
     times_table(weighted, filtered)
 
     @each_chunk
@@ -423,7 +437,9 @@
             result = jnp.where(column == k, jnp.sum(value, axis=1, keepdims=True), result)
         return result
 
-    sums[b] = in_columns([totals[k] for k in range(4)])
+    own = in_columns([totals[k] for k in range(4)])
+    own = jnp.concatenate([own, jnp.zeros((LANES - share, LANES), jnp.float32)], axis=0)
+    sums[b] = own.T[:8, :]
     each_batch(lambda bt: side_copy(3, bt, b).start())
 
     each_other(lambda peer, bt, st: out_copy(0, peer, bt, st, peer).wait_recv())
@@ -465,7 +481,17 @@
     total = batch_parts[0]
     for bt in range(1, batch):
         total = total + batch_parts[bt]
-    gate_sums[...] = total
+    gate_sums[...] = total[:3, :]
+
+    each_batch(lambda bt: side_copy(2, bt, bt).wait_recv())
+    for p in range(blocks):
+        for half in range(freqs // LANES):
+            lanes = slice(half * LANES, (half + 1) * LANES)
+            grad_spectrum[half, pl.ds(p, width, stride=blocks), :] = spectrum_landed[p, :, lanes].astype(jnp.float32)
+    each_batch(lambda bt: side_copy(3, bt, bt).wait_recv())
+    total = jnp.concatenate([sums[bt, :, :share] for bt in range(batch)], axis=1)
+    value_sums[...] = total[:3, :]
+    skip_sums[...] = total[3:4, :]
 
     each_seq(lambda st: part_copy(st, s).wait_send())
     for n in range(2):
@@ -473,8 +499,6 @@
         each_other(lambda peer, bt, st: in_copy(n, peer, bt, st, me).wait_send())
         each_other(lambda peer, bt, st: out_copy(n, peer, bt, st, me).wait_send())
     for n in range(5):
-        if n in (2, 3):
-            each_batch(lambda bt: side_copy(n, bt, bt).wait_recv())
         each_batch(lambda bt: side_copy(n, bt, b).wait_send())
     each_other(lambda peer, bt, st: out_copy(1, peer, bt, st, peer).wait_recv())
 
@@ -488,28 +512,34 @@
     share = channels // count
     blocks, block = mixing.shape[0], twiddle.shape[1]
     freqs = block // batch
-    params = jnp.concatenate([taps_values, taps_gates, skip_gain[None], skip_gain[None]], axis=0).T
     vmem = pl.BlockSpec(memory_space=pltpu.VMEM)
     hbm = pl.BlockSpec(memory_space=pl.ANY)
     smem = pl.BlockSpec(memory_space=pltpu.SMEM)
     field = jax.ShapeDtypeStruct((channels, length), jnp.bfloat16)
     rows = blocks * share
-    mixed, grad_values, grad_gates, grad_spectrum, sums, gate_sums = pl.pallas_call(
+    mixed, grad_values, grad_gates, grad_spectrum, value_sums, gate_sums, skip_sums = pl.pallas_call(
         functools.partial(whole_sequences, batch, seq),
         out_shape=[
             field, field, field,
-            jax.ShapeDtypeStruct((blocks, channels // seq, freqs), jnp.bfloat16),
-            jax.ShapeDtypeStruct((batch, share, LANES), jnp.float32),
-            jax.ShapeDtypeStruct((8, channels // seq), jnp.float32),
+            jax.ShapeDtypeStruct((freqs // LANES, blocks * channels // seq, LANES), jnp.float32),
+            jax.ShapeDtypeStruct((3, channels // seq), jnp.float32),
+            jax.ShapeDtypeStruct((3, channels // seq), jnp.float32),
+            jax.ShapeDtypeStruct((1, channels // seq), jnp.float32),
         ],
-        in_specs=[hbm, hbm, hbm, hbm, vmem, smem, vmem, hbm],
-        out_specs=[vmem] * 6,
+        in_specs=[hbm, hbm, hbm, hbm, vmem, smem, vmem, vmem, vmem, hbm],
+        out_specs=[vmem] * 7,
         scratch_shapes=[
             pltpu.VMEM((channels, length), jnp.bfloat16),
             pltpu.VMEM((channels, length), jnp.bfloat16),
             pltpu.VMEM((block, block), jnp.bfloat16),
+            pltpu.VMEM((channels, LANES), jnp.float32),
+            pltpu.VMEM((LANES, channels), jnp.float32),
+            pltpu.VMEM((batch, share, blocks, freqs), jnp.bfloat16),
+            pltpu.VMEM((freqs // LANES, share * blocks, LANES), jnp.float32),
+            pltpu.VMEM((blocks, channels // seq, freqs), jnp.bfloat16),
+            pltpu.VMEM((batch, 8, LANES), jnp.float32),
             pltpu.VMEM((2, count, share, length), jnp.bfloat16),
-            pltpu.VMEM((batch, blocks, share, freqs), jnp.bfloat16),
+            pltpu.VMEM((batch, blocks, share, freqs), jnp.float32),
             pltpu.VMEM((batch, blocks // batch, block), jnp.float32),
             pltpu.VMEM((rows, block), jnp.bfloat16),
             pltpu.VMEM((rows, block), jnp.bfloat16),
@@ -547,13 +577,13 @@
             collective_id=0, has_side_effects=True, vmem_limit_bytes=56 * 2**20
         ),
     )(
-        values, gates, cotangent, spectrum.transpose(1, 0, 2), twiddle, mixing, params,
-        cas_table(block),
-    )
-    sums = sums.reshape(channels // seq, LANES).T
-    grad_spectrum = grad_spectrum.transpose(1, 0, 2).astype(jnp.float32)
+        values, gates, cotangent, spectrum, twiddle, mixing, taps_values, taps_gates,
+        skip_gain[None], cas_table(block),
+    )
+    grad_spectrum = grad_spectrum.reshape(-1, channels // seq, blocks, LANES)
+    grad_spectrum = jnp.concatenate(list(grad_spectrum), axis=2)
     return (
-        mixed, grad_values, grad_gates, grad_spectrum, sums[:3], gate_sums[:3], sums[3]
+        mixed, grad_values, grad_gates, grad_spectrum, value_sums, gate_sums, skip_sums[0]
     )
 
 
@@ -570,6 +600,8 @@
         and block % length == 0
         and block % (batch * LANES) == 0
         and mixing.shape[0] % batch == 0
+        and mixing.shape[0] % 8 == 0
+        and channels // count <= LANES
     )
     return (per_device_kernel if fits else per_device_plain)(values, *rest)
 

time: 86 us -> 78.9 us (0.917)
  local copies, waits for them, and re-layouts: 10.3 us -> 5.4 us
  Pallas kernels: 72.7 us -> 70.9 us
  other arithmetic: 1.97 us -> 1.04 us
    slice x2 -> x0, local copies, waits for them, and re-layouts: 1.9 us -> none  [the longest x1 1.32 us: per_device_kernel(): gate_sums[:3]]
    unnamed x11 -> x18, local copies, waits for them, and re-layouts: 5.91 us -> 4.07 us
    pallas_call x1, Pallas kernels: 72.7 us -> 70.9 us  [per_device_kernel(): pl.pallas_call(functools.partial(whole_sequences, batch, seq), out_shape=...]
    another operation x0 -> x1, local copies, waits for them, and re-layouts: none -> 1.33 us  [per_device_kernel(): grad_spectrum = jnp.concatenate(list(grad_spectrum), axis=2)]
    convert_element_type x1 -> x0, other arithmetic: 1.18 us -> none  [per_device_kernel(): grad_spectrum = grad_spectrum.transpose(1, 0, 2).astype(jnp.float32)]
    concatenate x1 -> x0, local copies, waits for them, and re-layouts: 1 us -> none  [per_device_kernel(): jnp.concatenate([taps_values, taps_gates, skip_gain[None], skip_gain[None...]
    reshape x1 -> x0, local copies, waits for them, and re-layouts: 0.93 us -> none  [per_device_kernel(): sums = sums.reshape(channels // seq, LANES).T]
where the time goes in v3:
time: 78.9 us; the launch traced here: 78 us
  Pallas kernels  70.9 us (90%)
  local copies, waits for them, and re-layouts  5.4 us (7%)
  other arithmetic  1.04 us (1%)
    pallas_call x1, Pallas kernels, per_device_kernel(): pl.pallas_call(functools.partial(whole_sequences, batch, seq), out_shape=...  70.9 us
    unnamed x18, local copies, waits for them, and re-layouts  4.07 us

profile of v3, /device:TPU:0, one launch (start us, length us, event | category | flops | bytes accessed | tf_op | source)
XLA Modules:
  0.0 78.0 jit_solution(7049956790091605042)
XLA Ops:
  0.6 70.9 %shard_map.153 = (bf16[1024,256]{1,0:T(8,128)(2,1)}, bf16[1024,256]{1,0:T(8,128)(2,1)}, bf16[1024,256]{1,0:T(8,128)(2,1)}, f32[2,1024,128]{2,1,0:T(8,128)}, f32[...) custom-call(bf16[1024,256]{1,0:T(8,128)(2,1)} %values.1, bf16[1024,256]{1,0:T(8,128)(2,1)} %gates_in.1, ...), custom_call_target="tpu_custom_call" | custom-call | tf_op jit(solution)/shard_map/pallas_call | solution.py:520
  71.6 0.0 copy-start.2
  71.6 1.3 %slice_bitcast_fusion.1 = (f32[128,8,128]{2,1,0:T(8,128)S(1)}, f32[128,8,128]{2,1,0:T(8,128)S(1)}) fusion(f32[2,1024,128]{2,1,0:T(8,128)} %get-tuple-element.17), kind=kLoop, calls=%fused_computation.2 | loop fusion | bytes 2097152 | tf_op jit(solution)/shard_map/unstack | solution.py:584
  72.9 0.0 copy-start.1
  72.9 0.0 copy-start
  72.9 1.0 %pad_maximum_fusion = f32[128,8,256]{2,1,0:T(8,128)} fusion(f32[128,8,128]{2,1,0:T(8,128)S(1)} %get-tuple-element.22, f32[128,8,128]{2,1,0:T(8,128)S(1)} %get-tuple-element.21), kind=kLoop, calls=%fused_computation | loop fusion | flops 262144 | bytes 2097152 | tf_op jit(solution)/shard_map/concatenate | solution.py:584
  74.0 0.0 copy-done.2
  74.0 0.0 copy-start.4
  74.0 0.0 copy-start.3
  74.0 0.0 copy-start.5
  74.0 0.8 %copy.23 = bf16[1024,256]{1,0:T(8,128)(2,1)} copy(bf16[1024,256]{1,0:T(8,128)(2,1)S(1)} %copy-done.2) | data formatting | bytes 1048576
  74.8 0.0 copy-done.1
  74.8 0.8 %copy.24 = bf16[1024,256]{1,0:T(8,128)(2,1)} copy(bf16[1024,256]{1,0:T(8,128)(2,1)S(1)} %copy-done.1) | data formatting | bytes 1048576
  75.6 0.0 copy-done
  75.6 0.8 %copy.25 = bf16[1024,256]{1,0:T(8,128)(2,1)} copy(bf16[1024,256]{1,0:T(8,128)(2,1)S(1)} %copy-done) | data formatting | bytes 1048576
  76.4 0.0 copy-done.4
  76.4 0.6 copy.26
  76.9 0.0 copy-done.3
  76.9 0.6 copy.27
  77.5 0.0 copy-done.5
  77.5 0.5 copy.28
Async XLA Ops:
  71.6 2.4 %copy-start.2 = (bf16[1024,256]{1,0:T(8,128)(2,1)S(1)}, bf16[1024,256]{1,0:T(8,128)(2,1)}, u32[]{:S(2)}) copy-start(bf16[1024,256]{1,0:T(8,128)(2,1)} %get-tuple-element.30) | copy-start | bytes 1572868
  72.9 1.9 %copy-start.1 = (bf16[1024,256]{1,0:T(8,128)(2,1)S(1)}, bf16[1024,256]{1,0:T(8,128)(2,1)}, u32[]{:S(2)}) copy-start(bf16[1024,256]{1,0:T(8,128)(2,1)} %get-tuple-element.31) | copy-start | bytes 1572868
  72.9 2.7 %copy-start = (bf16[1024,256]{1,0:T(8,128)(2,1)S(1)}, bf16[1024,256]{1,0:T(8,128)(2,1)}, u32[]{:S(2)}) copy-start(bf16[1024,256]{1,0:T(8,128)(2,1)} %get-tuple-element.32) | copy-start | bytes 1572868
  74.0 2.4 %copy-start.4 = (f32[3,128]{1,0:T(4,128)S(1)}, f32[3,128]{1,0:T(4,128)}, u32[]{:S(2)}) copy-start(f32[3,128]{1,0:T(4,128)} %get-tuple-element.34) | copy-start | bytes 4612
  74.0 3.0 %copy-start.3 = (f32[3,128]{1,0:T(4,128)S(1)}, f32[3,128]{1,0:T(4,128)}, u32[]{:S(2)}) copy-start(f32[3,128]{1,0:T(4,128)} %get-tuple-element.35) | copy-start | bytes 4612
  74.0 3.6 %copy-start.5 = (f32[1,128]{1,0:T(1,128)S(1)}, f32[1,128]{1,0:T(1,128)}, u32[]{:S(2)}) copy-start(f32[1,128]{1,0:T(1,128)} %get-tuple-element.20) | copy-start | bytes 1540

commit v4 on v3

--- a/solution.py
+++ b/solution.py
@@ -113,7 +113,7 @@
     batch, seq,
     values, gates_in, cotangent_in, spectrum, twiddle, mixing, value_taps_in, gate_taps_in, skip_in, cas_in,
     mixed, grad_values, grad_gates, grad_spectrum, value_sums, gate_sums, skip_sums,
-    gates, cotangent, cas, params, turned_params, filters_landed, unpacked, spectrum_landed, sums,
+    gates, cotangent, cas, params, turned_params, filters_landed, unpacked, spectrum_landed, sums, turned_spectrum,
     fields, filters, factors, short_values, grad_long, wide, weighted,
     spectra, filtered, gradient, out_fields, out_spectrum, totals,
     short_gates, long_here, inner_here, gates_gradient, before, after, rims, line, parts, batch_parts,
@@ -173,22 +173,22 @@
     rims[0] = gates[:, length - LANES :].astype(jnp.float32).T[LANES - 8 :, :]
     pl.semaphore_wait(barrier, count - 1)
 
-    def in_copy(n, peer, bt, st, slot):
+    def in_copy(n, peer, bt, st):
         return pltpu.make_async_remote_copy(
             src_ref=(values, long_here)[n].at[rows_of(bt, st), :],
             dst_ref=fields.at[n, me],
-            send_sem=in_send.at[n, peer],
-            recv_sem=in_recv.at[n, slot],
+            send_sem=in_send.at[n],
+            recv_sem=in_recv.at[n],
             device_id=(bt, st),
             device_id_type=MESH,
         )
 
-    def out_copy(n, peer, bt, st, slot):
+    def out_copy(n, peer, bt, st):
         return pltpu.make_async_remote_copy(
             src_ref=out_fields.at[n, peer],
             dst_ref=(inner_here, grad_values)[n].at[rows_of(b, s), :],
-            send_sem=out_send.at[n, peer],
-            recv_sem=out_recv.at[n, slot],
+            send_sem=out_send.at[n],
+            recv_sem=out_recv.at[n],
             device_id=(bt, st),
             device_id_type=MESH,
         )
@@ -237,13 +237,17 @@
             body(lax.rem(s + step, seq))
 
     def start_in(n):
-        each_other(lambda peer, bt, st: in_copy(n, peer, bt, st, me).start())
+        each_other(lambda peer, bt, st: in_copy(n, peer, bt, st).start())
+
+    def wait_all(buffer, semaphore):
+        pieces = buffer.at[pl.ds(0, count - 1)]
+        pltpu.make_async_copy(pieces, pieces, semaphore).wait()
 
     def wait_in(n):
-        each_other(lambda peer, bt, st: in_copy(n, peer, bt, st, peer).wait_recv())
+        wait_all(fields.at[n], in_recv.at[n])
 
     def start_out(n):
-        each_other(lambda peer, bt, st: out_copy(n, peer, bt, st, me).start())
+        each_other(lambda peer, bt, st: out_copy(n, peer, bt, st).start())
         (inner_here, grad_values)[n][rows_of(b, s), :] = out_fields[n, me]
 
     rim_copy(0).start()
@@ -419,6 +423,32 @@
 
     start_out(1)
 
+    column = lax.broadcasted_iota(jnp.int32, (share, LANES), 1)
+
+    def in_columns(columns):
+        result = jnp.zeros((share, LANES), jnp.float32)
+        for k, value in enumerate(columns):
+            result = jnp.where(column == k, jnp.sum(value, axis=1, keepdims=True), result)
+        return result
+
+    wait_all(out_fields.at[0], out_recv.at[0])
+
+    @each_group
+    def _(rows):
+        inner = inner_here[rows, :].astype(jnp.float32)
+        mixed[rows, :] = (short_gates[rows, :] * inner).astype(mixed.dtype)
+        grads = cotangent[rows, :].astype(jnp.float32) * inner
+        gates_gradient[rows, :] = grads
+        shifted = delayed_by(gates[rows, :].astype(jnp.float32), before[rows, :])
+        line[rows, :] = in_columns([grads * shifted[k] for k in range(3)])
+
+    rims[1] = gates_gradient[:, :LANES].T[:8, :]
+    rim_copy(1).start()
+    turned = line[...].T[:8, :]
+    for st in range(seq):
+        parts[0, st] = turned[:, st * width : (st + 1) * width]
+    each_seq(lambda st: part_copy(st, s).start())
+    parts[1, s] = parts[0, s]
     @each_chunk
     def _(d, rows, columns):
         shifted = delays(d)
@@ -429,37 +459,11 @@
             rows, columns
         ].astype(jnp.float32)
 
-    column = lax.broadcasted_iota(jnp.int32, (share, LANES), 1)
-
-    def in_columns(columns):
-        result = jnp.zeros((share, LANES), jnp.float32)
-        for k, value in enumerate(columns):
-            result = jnp.where(column == k, jnp.sum(value, axis=1, keepdims=True), result)
-        return result
-
     own = in_columns([totals[k] for k in range(4)])
     own = jnp.concatenate([own, jnp.zeros((LANES - share, LANES), jnp.float32)], axis=0)
     sums[b] = own.T[:8, :]
     each_batch(lambda bt: side_copy(3, bt, b).start())
 
-    each_other(lambda peer, bt, st: out_copy(0, peer, bt, st, peer).wait_recv())
-
-    @each_group
-    def _(rows):
-        inner = inner_here[rows, :].astype(jnp.float32)
-        mixed[rows, :] = (short_gates[rows, :] * inner).astype(mixed.dtype)
-        grads = cotangent[rows, :].astype(jnp.float32) * inner
-        gates_gradient[rows, :] = grads
-        shifted = delayed_by(gates[rows, :].astype(jnp.float32), before[rows, :])
-        line[rows, :] = in_columns([grads * shifted[k] for k in range(3)])
-
-    rims[1] = gates_gradient[:, :LANES].T[:8, :]
-    rim_copy(1).start()
-    turned = line[...].T[:8, :]
-    for st in range(seq):
-        parts[0, st] = turned[:, st * width : (st + 1) * width]
-    each_seq(lambda st: part_copy(st, s).start())
-    parts[1, s] = parts[0, s]
     rim_copy(1).wait_recv()
     came = jnp.where(me < count - 1, rims[3], 0.0)
     padded = jnp.concatenate([came, jnp.zeros((LANES - 8, came.shape[1]), jnp.float32)], axis=0)
@@ -471,6 +475,13 @@
         shifted = advanced_by(gates_gradient[rows, :], after[rows, :])
         grad_gates[rows, :] = conv(gate_taps(rows), shifted).astype(grad_gates.dtype)
 
+    each_batch(lambda bt: side_copy(2, bt, bt).wait_recv())
+    for p in range(blocks):
+        for half in range(freqs // LANES):
+            lanes = slice(half * LANES, (half + 1) * LANES)
+            turned_spectrum[half, pl.ds(p, width, stride=blocks), :] = spectrum_landed[p, :, lanes].astype(jnp.float32)
+    for half in range(freqs // LANES):
+        grad_spectrum[:, half * LANES : (half + 1) * LANES] = turned_spectrum[half]
     each_seq(lambda st: part_copy(st, st).wait_recv())
     total = parts[1, 0]
     for st in range(1, seq):
@@ -483,11 +494,6 @@
         total = total + batch_parts[bt]
     gate_sums[...] = total[:3, :]
 
-    each_batch(lambda bt: side_copy(2, bt, bt).wait_recv())
-    for p in range(blocks):
-        for half in range(freqs // LANES):
-            lanes = slice(half * LANES, (half + 1) * LANES)
-            grad_spectrum[half, pl.ds(p, width, stride=blocks), :] = spectrum_landed[p, :, lanes].astype(jnp.float32)
     each_batch(lambda bt: side_copy(3, bt, bt).wait_recv())
     total = jnp.concatenate([sums[bt, :, :share] for bt in range(batch)], axis=1)
     value_sums[...] = total[:3, :]
@@ -496,11 +502,11 @@
     each_seq(lambda st: part_copy(st, s).wait_send())
     for n in range(2):
         rim_copy(n).wait_send()
-        each_other(lambda peer, bt, st: in_copy(n, peer, bt, st, me).wait_send())
-        each_other(lambda peer, bt, st: out_copy(n, peer, bt, st, me).wait_send())
+        wait_all(fields.at[n], in_send.at[n])
+        wait_all(out_fields.at[n], out_send.at[n])
     for n in range(5):
         each_batch(lambda bt: side_copy(n, bt, b).wait_send())
-    each_other(lambda peer, bt, st: out_copy(1, peer, bt, st, peer).wait_recv())
+    wait_all(out_fields.at[1], out_recv.at[1])
 
 
 def per_device_kernel(
@@ -521,7 +527,7 @@
         functools.partial(whole_sequences, batch, seq),
         out_shape=[
             field, field, field,
-            jax.ShapeDtypeStruct((freqs // LANES, blocks * channels // seq, LANES), jnp.float32),
+            jax.ShapeDtypeStruct((blocks * channels // seq, freqs), jnp.float32),
             jax.ShapeDtypeStruct((3, channels // seq), jnp.float32),
             jax.ShapeDtypeStruct((3, channels // seq), jnp.float32),
             jax.ShapeDtypeStruct((1, channels // seq), jnp.float32),
@@ -538,6 +544,7 @@
             pltpu.VMEM((freqs // LANES, share * blocks, LANES), jnp.float32),
             pltpu.VMEM((blocks, channels // seq, freqs), jnp.bfloat16),
             pltpu.VMEM((batch, 8, LANES), jnp.float32),
+            pltpu.VMEM((freqs // LANES, blocks * channels // seq, LANES), jnp.float32),
             pltpu.VMEM((2, count, share, length), jnp.bfloat16),
             pltpu.VMEM((batch, blocks, share, freqs), jnp.float32),
             pltpu.VMEM((batch, blocks // batch, block), jnp.float32),
@@ -561,10 +568,10 @@
             pltpu.VMEM((channels, LANES), jnp.float32),
             pltpu.VMEM((2, seq, 8, channels // seq), jnp.float32),
             pltpu.VMEM((batch, 8, channels // seq), jnp.float32),
-            pltpu.SemaphoreType.DMA((2, count)),
-            pltpu.SemaphoreType.DMA((2, count)),
-            pltpu.SemaphoreType.DMA((2, count)),
-            pltpu.SemaphoreType.DMA((2, count)),
+            pltpu.SemaphoreType.DMA((2,)),
+            pltpu.SemaphoreType.DMA((2,)),
+            pltpu.SemaphoreType.DMA((2,)),
+            pltpu.SemaphoreType.DMA((2,)),
             pltpu.SemaphoreType.DMA((5, batch)),
             pltpu.SemaphoreType.DMA((5, batch)),
             pltpu.SemaphoreType.DMA((2,)),
@@ -580,8 +587,7 @@
         values, gates, cotangent, spectrum, twiddle, mixing, taps_values, taps_gates,
         skip_gain[None], cas_table(block),
     )
-    grad_spectrum = grad_spectrum.reshape(-1, channels // seq, blocks, LANES)
-    grad_spectrum = jnp.concatenate(list(grad_spectrum), axis=2)
+    grad_spectrum = grad_spectrum.reshape(channels // seq, blocks, freqs)
     return (
         mixed, grad_values, grad_gates, grad_spectrum, value_sums, gate_sums, skip_sums[0]
     )

time: 78.9 us -> 74.6 us (0.946)
  Pallas kernels: 70.9 us -> 66 us
  local copies, waits for them, and re-layouts: 5.4 us -> 7.31 us
  other arithmetic: 1.04 us -> 0 us
    pallas_call x1, Pallas kernels: 70.9 us -> 66 us  [per_device_kernel(): pl.pallas_call(functools.partial(whole_sequences, batch, seq), out_shape=...]
    unnamed x18 -> x17, local copies, waits for them, and re-layouts: 4.07 us -> 7.31 us
    another operation x1 -> x0, local copies, waits for them, and re-layouts: 1.33 us -> none  [per_device_kernel(): grad_spectrum = jnp.concatenate(list(grad_spectrum), axis=2)]
    concatenate x1 -> x0, other arithmetic: 1.04 us -> none  [per_device_kernel(): grad_spectrum = jnp.concatenate(list(grad_spectrum), axis=2)]
where the time goes in v4:
time: 74.6 us; the launch traced here: 73.9 us
  Pallas kernels  66 us (88%)
  local copies, waits for them, and re-layouts  7.31 us (10%)
    pallas_call x1, Pallas kernels, per_device_kernel(): pl.pallas_call(functools.partial(whole_sequences, batch, seq), out_shape=...  66 us
    unnamed x17, local copies, waits for them, and re-layouts  7.31 us

profile of v4, /device:TPU:0, one launch (start us, length us, event | category | flops | bytes accessed | tf_op | source)
XLA Modules:
  0.0 73.9 jit_solution(7960338419622819141)
XLA Ops:
  0.6 66.0 %shard_map.153 = (bf16[1024,256]{1,0:T(8,128)(2,1)}, bf16[1024,256]{1,0:T(8,128)(2,1)}, bf16[1024,256]{1,0:T(8,128)(2,1)}, f32[1024,256]{1,0:T(8,128)}, f32[3,12...) custom-call(bf16[1024,256]{1,0:T(8,128)(2,1)} %values.1, bf16[1024,256]{1,0:T(8,128)(2,1)} %gates_in.1, ...), custom_call_target="tpu_custom_call" | custom-call | tf_op jit(solution)/shard_map/pallas_call | solution.py:526
  66.6 0.0 copy-start.1
  66.6 0.0 copy-start
  66.6 2.0 %copy.24 = bf16[1024,256]{1,0:T(8,128)(2,1)} copy(bf16[1024,256]{1,0:T(8,128)(2,1)} %get-tuple-element.28) | data formatting | bytes 1048576
  68.6 0.0 copy-start.3
  68.6 0.0 copy-start.2
  68.6 0.0 copy-start.4
  68.6 1.9 %copy.25 = bf16[1024,256]{1,0:T(8,128)(2,1)} copy(bf16[1024,256]{1,0:T(8,128)(2,1)} %get-tuple-element.29) | data formatting | bytes 1048576
  70.5 0.0 copy-done.1
  70.5 0.8 %copy.26 = bf16[1024,256]{1,0:T(8,128)(2,1)} copy(bf16[1024,256]{1,0:T(8,128)(2,1)S(1)} %copy-done.1) | data formatting | bytes 1048576
  71.3 0.0 copy-done
  71.3 1.0 %copy.27 = f32[128,8,256]{2,1,0:T(8,128)} copy(f32[128,8,256]{2,1,0:T(8,128)S(1)} %bitcast.3) | data formatting | bytes 2097152
  72.3 0.0 copy-done.3
  72.3 0.6 copy.28
  72.8 0.0 copy-done.2
  72.8 0.6 copy.29
  73.4 0.0 copy-done.4
  73.4 0.5 copy.30
Async XLA Ops:
  66.6 3.9 %copy-start.1 = (bf16[1024,256]{1,0:T(8,128)(2,1)S(1)}, bf16[1024,256]{1,0:T(8,128)(2,1)}, u32[]{:S(2)}) copy-start(bf16[1024,256]{1,0:T(8,128)(2,1)} %get-tuple-element.30) | copy-start | bytes 1572868
  66.6 4.7 %copy-start = (f32[1024,256]{1,0:T(8,128)S(1)}, f32[1024,256]{1,0:T(8,128)}, u32[]{:S(2)}) copy-start(f32[1024,256]{1,0:T(8,128)} %get-tuple-element.17) | copy-start | bytes 3145732
  68.6 3.7 %copy-start.3 = (f32[3,128]{1,0:T(4,128)S(1)}, f32[3,128]{1,0:T(4,128)}, u32[]{:S(2)}) copy-start(f32[3,128]{1,0:T(4,128)} %get-tuple-element.32) | copy-start | bytes 4612
  68.6 4.2 %copy-start.2 = (f32[3,128]{1,0:T(4,128)S(1)}, f32[3,128]{1,0:T(4,128)}, u32[]{:S(2)}) copy-start(f32[3,128]{1,0:T(4,128)} %get-tuple-element.33) | copy-start | bytes 4612
  68.6 4.8 %copy-start.4 = (f32[1,128]{1,0:T(1,128)S(1)}, f32[1,128]{1,0:T(1,128)}, u32[]{:S(2)}) copy-start(f32[1,128]{1,0:T(1,128)} %get-tuple-element.20) | copy-start | bytes 1540

commit v5 on v4

--- a/solution.py
+++ b/solution.py
@@ -112,11 +112,11 @@
 def whole_sequences(
     batch, seq,
     values, gates_in, cotangent_in, spectrum, twiddle, mixing, value_taps_in, gate_taps_in, skip_in, cas_in,
-    mixed, grad_values, grad_gates, grad_spectrum, value_sums, gate_sums, skip_sums,
+    mixed_out, grad_values, grad_gates_out, grad_spectrum_out, value_sums, gate_sums, skip_sums,
     gates, cotangent, cas, params, turned_params, filters_landed, unpacked, spectrum_landed, sums, turned_spectrum,
     fields, filters, factors, short_values, grad_long, wide, weighted,
     spectra, filtered, gradient, out_fields, out_spectrum, totals,
-    short_gates, long_here, inner_here, gates_gradient, before, after, rims, line, parts, batch_parts,
+    mixed, grad_gates, grad_spectrum, short_gates, long_here, inner_here, gates_gradient, before, after, rims, line, parts, batch_parts,
     in_send, in_recv, out_send, out_recv, side_send, side_recv, rim_send, rim_recv,
     part_send, part_recv, local,
 ):
@@ -155,6 +155,13 @@
     load_filters = pltpu.make_async_copy(
         spectrum.at[batch_rows(b)], filters_landed.at[b], local.at[4]
     )
+
+    store_values = pltpu.make_async_copy(
+        out_fields.at[1, me], grad_values.at[rows_of(b, s), :], local.at[5]
+    )
+    store_mixed = pltpu.make_async_copy(mixed, mixed_out, local.at[6])
+    store_gates = pltpu.make_async_copy(grad_gates, grad_gates_out, local.at[7])
+    store_spectrum = pltpu.make_async_copy(grad_spectrum, grad_spectrum_out, local.at[8])
 
     barrier = pltpu.get_barrier_semaphore()
     each_other(lambda peer, bt, st: pl.semaphore_signal(
@@ -248,7 +255,6 @@
 
     def start_out(n):
         each_other(lambda peer, bt, st: out_copy(n, peer, bt, st).start())
-        (inner_here, grad_values)[n][rows_of(b, s), :] = out_fields[n, me]
 
     rim_copy(0).start()
     start_in(0)
@@ -399,6 +405,7 @@
         out_fields[0, d] = inner.astype(out_fields.dtype)
 
     start_out(0)
+    inner_here[rows_of(b, s), :] = out_fields[0, me]
 
     wait_in(1)
 
@@ -422,6 +429,7 @@
         out_fields[1, d] = conv(value_taps, advances(d)).astype(out_fields.dtype)
 
     start_out(1)
+    store_values.start()
 
     column = lax.broadcasted_iota(jnp.int32, (share, LANES), 1)
 
@@ -442,6 +450,7 @@
         shifted = delayed_by(gates[rows, :].astype(jnp.float32), before[rows, :])
         line[rows, :] = in_columns([grads * shifted[k] for k in range(3)])
 
+    store_mixed.start()
     rims[1] = gates_gradient[:, :LANES].T[:8, :]
     rim_copy(1).start()
     turned = line[...].T[:8, :]
@@ -475,6 +484,7 @@
         shifted = advanced_by(gates_gradient[rows, :], after[rows, :])
         grad_gates[rows, :] = conv(gate_taps(rows), shifted).astype(grad_gates.dtype)
 
+    store_gates.start()
     each_batch(lambda bt: side_copy(2, bt, bt).wait_recv())
     for p in range(blocks):
         for half in range(freqs // LANES):
@@ -482,6 +492,7 @@
             turned_spectrum[half, pl.ds(p, width, stride=blocks), :] = spectrum_landed[p, :, lanes].astype(jnp.float32)
     for half in range(freqs // LANES):
         grad_spectrum[:, half * LANES : (half + 1) * LANES] = turned_spectrum[half]
+    store_spectrum.start()
     each_seq(lambda st: part_copy(st, st).wait_recv())
     total = parts[1, 0]
     for st in range(1, seq):
@@ -506,7 +517,27 @@
         wait_all(out_fields.at[n], out_send.at[n])
     for n in range(5):
         each_batch(lambda bt: side_copy(n, bt, b).wait_send())
+    for store in (store_values, store_mixed, store_gates, store_spectrum):
+        store.wait()
     wait_all(out_fields.at[1], out_recv.at[1])
+
+
+def hand_over(*refs):
+    count = len(refs) // 2
+    sources, targets, semaphores = refs[:count], refs[count : 2 * count], refs[-1]
+    copies = []
+    for n, (source, target) in enumerate(zip(sources, targets)):
+        parts = 4 if source.shape[0] % 64 == 0 else 1
+        rows = source.shape[0] // parts
+        for part in range(parts):
+            at = pl.ds(part * rows, rows)
+            copies.append(
+                pltpu.make_async_copy(source.at[at], target.at[at], semaphores.at[n, part])
+            )
+    for copy in copies:
+        copy.start()
+    for copy in copies:
+        copy.wait()
 
 
 def per_device_kernel(
@@ -523,7 +554,7 @@
     smem = pl.BlockSpec(memory_space=pltpu.SMEM)
     field = jax.ShapeDtypeStruct((channels, length), jnp.bfloat16)
     rows = blocks * share
-    mixed, grad_values, grad_gates, grad_spectrum, value_sums, gate_sums, skip_sums = pl.pallas_call(
+    results = pl.pallas_call(
         functools.partial(whole_sequences, batch, seq),
         out_shape=[
             field, field, field,
@@ -533,7 +564,7 @@
             jax.ShapeDtypeStruct((1, channels // seq), jnp.float32),
         ],
         in_specs=[hbm, hbm, hbm, hbm, vmem, smem, vmem, vmem, vmem, hbm],
-        out_specs=[vmem] * 7,
+        out_specs=[hbm] * 4 + [vmem] * 3,
         scratch_shapes=[
             pltpu.VMEM((channels, length), jnp.bfloat16),
             pltpu.VMEM((channels, length), jnp.bfloat16),
@@ -558,6 +589,9 @@
             pltpu.VMEM((2, count, share, length), jnp.bfloat16),
             pltpu.VMEM((batch, blocks, share, freqs), jnp.bfloat16),
             pltpu.VMEM((4, share, length), jnp.float32),
+            pltpu.VMEM((channels, length), jnp.bfloat16),
+            pltpu.VMEM((channels, length), jnp.bfloat16),
+            pltpu.VMEM((blocks * channels // seq, freqs), jnp.float32),
             pltpu.VMEM((channels, length), jnp.float32),
             pltpu.VMEM((channels, length), jnp.bfloat16),
             pltpu.VMEM((channels, length), jnp.bfloat16),
@@ -578,7 +612,7 @@
             pltpu.SemaphoreType.DMA((2,)),
             pltpu.SemaphoreType.DMA((seq,)),
             pltpu.SemaphoreType.DMA((seq,)),
-            pltpu.SemaphoreType.DMA((5,)),
+            pltpu.SemaphoreType.DMA((9,)),
         ],
         compiler_params=pltpu.CompilerParams(
             collective_id=0, has_side_effects=True, vmem_limit_bytes=56 * 2**20
@@ -587,6 +621,14 @@
         values, gates, cotangent, spectrum, twiddle, mixing, taps_values, taps_gates,
         skip_gain[None], cas_table(block),
     )
+    mixed, grad_values, grad_gates, grad_spectrum, value_sums, gate_sums, skip_sums = pl.pallas_call(
+        hand_over,
+        out_shape=[jax.ShapeDtypeStruct(one.shape, one.dtype) for one in results],
+        in_specs=[hbm] * len(results),
+        out_specs=[hbm] * len(results),
+        scratch_shapes=[pltpu.SemaphoreType.DMA((len(results), 4))],
+        compiler_params=pltpu.CompilerParams(vmem_limit_bytes=56 * 2**20),
+    )(*results)
     grad_spectrum = grad_spectrum.reshape(channels // seq, blocks, freqs)
     return (
         mixed, grad_values, grad_gates, grad_spectrum, value_sums, gate_sums, skip_sums[0]

time: 74.6 us -> 147 us (1.97)
  Pallas kernels: 66 us -> 146 us
  local copies, waits for them, and re-layouts: 7.31 us -> 0 us
    pallas_call x0 -> x1, Pallas kernels: none -> 80.9 us  [per_device_kernel(): pl.pallas_call(hand_over, out_shape=[jax.ShapeDtypeStruct(one.shape, one....]
    unnamed x17 -> x0, local copies, waits for them, and re-layouts: 7.31 us -> none
where the time goes in v5:
time: 147 us
  Pallas kernels  146 us (99%)
    pallas_call x1, Pallas kernels, per_device_kernel(): pl.pallas_call(hand_over, out_shape=[jax.ShapeDtypeStruct(one.shape, one....  80.9 us
    pallas_call x1, Pallas kernels, per_device_kernel(): pl.pallas_call(functools.partial(whole_sequences, batch, seq), out_shape=...  65.1 us

profile of v5, /device:TPU:0, one launch (start us, length us, event | category | flops | bytes accessed | tf_op | source)
XLA Modules:
  0.0 146.7 jit_solution(12594874720594969860)
XLA Ops:
  0.6 65.1 %shard_map.153 = (bf16[1024,256]{1,0:T(8,128)(2,1)}, bf16[1024,256]{1,0:T(8,128)(2,1)}, bf16[1024,256]{1,0:T(8,128)(2,1)}, f32[1024,256]{1,0:T(8,128)}, f32[3,12...) custom-call(bf16[1024,256]{1,0:T(8,128)(2,1)} %values.1, bf16[1024,256]{1,0:T(8,128)(2,1)} %gates_in.1, ...), custom_call_target="tpu_custom_call" | custom-call | tf_op jit(solution)/shard_map/pallas_call | solution.py:557
  65.8 80.9 %shard_map.154 = (bf16[1024,256]{1,0:T(8,128)(2,1)}, bf16[1024,256]{1,0:T(8,128)(2,1)}, bf16[1024,256]{1,0:T(8,128)(2,1)}, f32[1024,256]{1,0:T(8,128)}, f32[3,12...) custom-call(bf16[1024,256]{1,0:T(8,128)(2,1)} %get-tuple-element.21.refs_0_, ...), custom_call_target="tpu_custom_call" | custom-call | tf_op jit(solution)/shard_map/pallas_call | solution.py:624

commit v6 on v5

--- a/solution.py
+++ b/solution.py
@@ -522,22 +522,26 @@
     wait_all(out_fields.at[1], out_recv.at[1])
 
 
-def hand_over(*refs):
-    count = len(refs) // 2
-    sources, targets, semaphores = refs[:count], refs[count : 2 * count], refs[-1]
-    copies = []
+def hand_over(count, *refs):
+    sources, targets, held = refs[:count], refs[count : 2 * count], refs[2 * count : 3 * count]
+    arrive, leave = refs[3 * count :]
+    steps = []
     for n, (source, target) in enumerate(zip(sources, targets)):
         parts = 4 if source.shape[0] % 64 == 0 else 1
         rows = source.shape[0] // parts
         for part in range(parts):
             at = pl.ds(part * rows, rows)
-            copies.append(
-                pltpu.make_async_copy(source.at[at], target.at[at], semaphores.at[n, part])
-            )
-    for copy in copies:
-        copy.start()
-    for copy in copies:
-        copy.wait()
+            steps.append((
+                pltpu.make_async_copy(source.at[at], held[n].at[at], arrive.at[n, part]),
+                pltpu.make_async_copy(held[n].at[at], target.at[at], leave.at[n, part]),
+            ))
+    for come, _ in steps:
+        come.start()
+    for come, go in steps:
+        come.wait()
+        go.start()
+    for _, go in steps:
+        go.wait()
 
 
 def per_device_kernel(
@@ -622,11 +626,12 @@
         skip_gain[None], cas_table(block),
     )
     mixed, grad_values, grad_gates, grad_spectrum, value_sums, gate_sums, skip_sums = pl.pallas_call(
-        hand_over,
+        functools.partial(hand_over, len(results)),
         out_shape=[jax.ShapeDtypeStruct(one.shape, one.dtype) for one in results],
         in_specs=[hbm] * len(results),
         out_specs=[hbm] * len(results),
-        scratch_shapes=[pltpu.SemaphoreType.DMA((len(results), 4))],
+        scratch_shapes=[pltpu.VMEM(one.shape, one.dtype) for one in results]
+        + [pltpu.SemaphoreType.DMA((len(results), 4))] * 2,
         compiler_params=pltpu.CompilerParams(vmem_limit_bytes=56 * 2**20),
     )(*results)
     grad_spectrum = grad_spectrum.reshape(channels // seq, blocks, freqs)

time: 147 us -> 69.5 us (0.47)
  Pallas kernels: 146 us -> 68.1 us
    pallas_call x1, Pallas kernels: 80.9 us -> 2.99 us  [per_device_kernel(): pl.pallas_call(functools.partial(hand_over, len(results)), out_shape=[jax...]
where the time goes in v6:
time: 69.5 us; the launch traced here: 68.8 us
  Pallas kernels  68.1 us (98%)
    pallas_call x1, Pallas kernels, per_device_kernel(): pl.pallas_call(functools.partial(whole_sequences, batch, seq), out_shape=...  65.1 us
    pallas_call x1, Pallas kernels, per_device_kernel(): pl.pallas_call(functools.partial(hand_over, len(results)), out_shape=[jax...  2.99 us

profile of v6, /device:TPU:0, one launch (start us, length us, event | category | flops | bytes accessed | tf_op | source)
XLA Modules:
  0.0 68.8 jit_solution(10294624256246833215)
XLA Ops:
  0.6 65.1 %shard_map.153 = (bf16[1024,256]{1,0:T(8,128)(2,1)}, bf16[1024,256]{1,0:T(8,128)(2,1)}, bf16[1024,256]{1,0:T(8,128)(2,1)}, f32[1024,256]{1,0:T(8,128)}, f32[3,12...) custom-call(bf16[1024,256]{1,0:T(8,128)(2,1)} %values.1, bf16[1024,256]{1,0:T(8,128)(2,1)} %gates_in.1, ...), custom_call_target="tpu_custom_call" | custom-call | tf_op jit(solution)/shard_map/pallas_call | solution.py:561
  65.8 3.0 %shard_map.154 = (bf16[1024,256]{1,0:T(8,128)(2,1)}, bf16[1024,256]{1,0:T(8,128)(2,1)}, bf16[1024,256]{1,0:T(8,128)(2,1)}, f32[1024,256]{1,0:T(8,128)}, f32[3,12...) custom-call(bf16[1024,256]{1,0:T(8,128)(2,1)} %get-tuple-element.21.refs_0_, ...), custom_call_target="tpu_custom_call" | custom-call | tf_op jit(solution)/shard_map/pallas_call | solution.py:628
